TPU v7x, 32 devices: a whole 2x2x4 slice. The times are simulated.
32 devices in a mesh: dp: 8 (over z, y), tensor: 4 (over x, core).
Axes of the slice: x: 2, y: 2, z: 4, core: 2. Of those that a mesh axis runs over, the one named last changes fastest.
Arguments:
- residual: bfloat16 [512, 8192], P('tensor'), may hold values from -120 to 120
- hidden_cotangent: bfloat16 [512, 14336], P('tensor', 'dp'), may hold values from -6 to 6
- norm_gain: float32 [8192], replicated, may hold values from 0.1 to 1.9
- gate_weight: bfloat16 [14336, 8192], P('dp', 'tensor'), may hold values from -0.0625 to 0.0625
- up_weight: bfloat16 [14336, 8192], P('dp', 'tensor'), may hold values from -0.0625 to 0.0625
Outputs:
- input_grad: bfloat16 [512, 8192], P('dp', 'tensor')
- gate_grad: bfloat16 [14336, 8192], P('dp', 'tensor')
- up_grad: bfloat16 [14336, 8192], P('dp', 'tensor')
- gain_grad: float32 [8192], P('tensor')
All inputs are finite; a program needn't handle non-finite values.
Results may differ from a plain program's by a relative error of at most 0.0085.
Values may be sent and summed in bfloat16 or wider, within the bound.
A program may use at most 192 MiB of HBM per device.

v0:
```python
import jax
import jax.numpy as jnp
from jax import lax
from jax.sharding import PartitionSpec as P


def activate(gate, up_proj, cotangent):
    cot_f = cotangent.astype(jnp.float32)
    sig = jax.nn.sigmoid(gate)
    gate_delta = (cot_f * up_proj * sig * (1.0 + gate * (1.0 - sig))).astype(jnp.bfloat16)
    up_delta = (cot_f * gate * sig).astype(jnp.bfloat16)
    return (gate_delta, up_delta)


def right_product(left, weight):
    return lax.dot_general(
        left, weight, (((1,), (1,)), ((), ())), preferred_element_type=jnp.float32
    )


def left_product(left, right):
    return lax.dot_general(
        left, right, (((0,), (0,)), ((), ())), preferred_element_type=jnp.float32
    )


def shards(residual, hidden_cotangent, norm_gain, gate_weight, up_weight):
    width = residual.shape[1]
    slice_width = gate_weight.shape[1]
    resid_f = residual.astype(jnp.float32)
    own_inv = lax.rsqrt(jnp.mean(resid_f * resid_f, axis=-1, keepdims=True) + 1e-05)
    normed = (resid_f * own_inv * norm_gain).astype(jnp.bfloat16)
    gate = right_product(normed, lax.all_gather(gate_weight, "tensor", axis=1, tiled=True))
    up_proj = right_product(normed, lax.all_gather(up_weight, "tensor", axis=1, tiled=True))
    gate_delta, up_delta = activate(gate, up_proj, hidden_cotangent)
    gate_all, up_all = (
        lax.all_gather(gate_delta, "tensor", axis=0, tiled=True),
        lax.all_gather(up_delta, "tensor", axis=0, tiled=True),
    )
    feat_resid = lax.all_to_all(residual, "tensor", split_axis=1, concat_axis=0, tiled=True)
    feat_f = feat_resid.astype(jnp.float32)
    squares_total = lax.psum(jnp.sum(feat_f * feat_f, axis=1), "tensor")
    feat_inv = lax.rsqrt(squares_total / width + 1e-05)[:, None]
    gain_slice = lax.dynamic_slice_in_dim(
        norm_gain, lax.axis_index("tensor") * slice_width, slice_width
    )
    feat_normed = (feat_f * feat_inv * gain_slice).astype(jnp.bfloat16)
    tokens_total = residual.shape[0] * lax.axis_size("tensor")
    scale = tokens_total ** (-0.5)
    gate_grad = (left_product(gate_all, feat_normed) * scale).astype(jnp.bfloat16)
    up_grad = (left_product(up_all, feat_normed) * scale).astype(jnp.bfloat16)
    rows_each = gate_all.shape[0] // lax.axis_size("dp")
    delta_rows = lax.psum_scatter(
        jnp.dot(gate_all, gate_weight, preferred_element_type=jnp.float32)
        + jnp.dot(up_all, up_weight, preferred_element_type=jnp.float32),
        "dp",
        scatter_dimension=0,
        tiled=True,
    )
    delta_f = delta_rows.astype(jnp.bfloat16).astype(jnp.float32)
    row_start = lax.axis_index("dp") * rows_each
    resid_rows = lax.dynamic_slice_in_dim(feat_f, row_start, rows_each, 0)
    inv_rows = lax.dynamic_slice_in_dim(feat_inv, row_start, rows_each, 0)
    gain_part = jnp.sum(delta_f * resid_rows * inv_rows, axis=0)
    coeff_part = jnp.sum(gain_slice * delta_f * resid_rows, axis=1)
    coeff = lax.psum(coeff_part, "tensor")[:, None] / width
    gain_total = lax.psum(gain_part, "dp")
    input_grad = (
        inv_rows * gain_slice * delta_f - resid_rows * (inv_rows * inv_rows * inv_rows) * coeff
    )
    return (input_grad.astype(jnp.bfloat16), gate_grad, up_grad, gain_total * scale)


def solution(mesh):
    return jax.shard_map(
        shards,
        mesh=mesh,
        in_specs=(P("tensor", None), P("tensor", "dp"), P(), P("dp", "tensor"), P("dp", "tensor")),
        out_specs=(P("dp", "tensor"), P("dp", "tensor"), P("dp", "tensor"), P("tensor")),
        check_vma=False,
    )
```

profile of v0, /device:TPU:0, one launch (start us, length us, event | category | flops | bytes accessed | tf_op | source)
XLA Modules:
  0.0 566.6 jit_solution(10561955230577809649)
XLA Ops:
  7.2 0.7 all-gather.7.cloned.1.call-update
  8.0 0.7 all-gather.5.cloned.1.call-update
  8.7 0.8 copy-done
  10.0 180.3 %all-gather.7.cloned.1.call-done = bf16[1792,8192]{1,0:T(8,128)(2,1)} async-done(((bf16[1792,2048]{1,0:T(8,128)(2,1)}), bf16[1792,8192]{1,0:T(8,128)(2,1)}) %all-gather.7.cloned.1.call-update) | async-done | bytes 29360144 | tf_op jit(solution)/shard_map/all_gather | solution.py:33
  190.3 17.9 %fusion.7 = (bf16[128,1792]{1,0:T(8,128)(2,1)}, f32[128,1792]{1,0:T(8,128)S(1)}) fusion(bf16[128,1792]{1,0:T(8,128)(2,1)S(1)} %copy-done.4, bf16[1792,8192]{1,0:T(8,128)(2,1)} %all-gather.7.cloned.1.call-done, bf16[128,8192]{1,0:T(8,128)(2,1)S(1)} %copy-done, f32[8192]{0:T(1024)S(1)} %copy-done.1, f32[128]{0:T(128)S(1)} %add_rsqrt_fusion.1), kind=kOutput, calls=%fused_computation.17 | convolution fusion | flops 3763896320 | bytes 33325568 | tf_op jit(solution)/shard_map/dot_general | solution.py:16
  208.2 161.7 %all-gather.5.cloned.1.call-done = bf16[1792,8192]{1,0:T(8,128)(2,1)} async-done(((bf16[1792,2048]{1,0:T(8,128)(2,1)}), bf16[1792,8192]{1,0:T(8,128)(2,1)}) %all-gather.5.cloned.1.call-update) | async-done | bytes 29360144 | tf_op jit(solution)/shard_map/all_gather | solution.py:34
  369.9 15.4 %fusion.5 = bf16[128,1792]{1,0:T(8,128)(2,1)} fusion(bf16[1792,8192]{1,0:T(8,128)(2,1)} %all-gather.5.cloned.1.call-done, bf16[128,1792]{1,0:T(8,128)(2,1)S(1)} %copy-done.4, f32[128,1792]{1,0:T(8,128)S(1)} %get-tuple-element.11, bf16[128,8192]{1,0:T(8,128)(2,1)S(1)} %copy-done, f32[8192]{0:T(1024)S(1)} %copy-done.1, f32[128]{0:T(128)S(1)} %add_rsqrt_fusion.1), kind=kOutput, calls=%fused_computation.13 | convolution fusion | flops 3764813824 | bytes 33325568 | tf_op jit(solution)/shard_map/dot_general | solution.py:16
  386.0 20.7 %all-gather.9.cloned.1.call-done = bf16[512,1792]{1,0:T(8,128)(2,1)} async-done(((bf16[128,1792]{1,0:T(8,128)(2,1)}), bf16[512,1792]{1,0:T(8,128)(2,1)}) %all-gather.9.cloned.1.call-update) | async-done | bytes 1835024 | tf_op jit(solution)/shard_map/all_gather | solution.py:37
  406.7 9.6 %fusion.17 = f32[512,2048]{1,0:T(8,128)} fusion(bf16[512,1792]{1,0:T(8,128)(2,1)} %all-gather.9.cloned.1.call-done, bf16[1792,2048]{1,0:T(8,128)(2,1)} %param.8), kind=kOutput, calls=%fused_computation.34 | convolution fusion | flops 3758096384 | bytes 13369344 | tf_op jit(solution)/shard_map/dot_general | solution.py:54
  416.3 13.5 %all-gather.11.cloned.1.call-done = bf16[512,1792]{1,0:T(8,128)(2,1)} async-done(((bf16[128,1792]{1,0:T(8,128)(2,1)}), bf16[512,1792]{1,0:T(8,128)(2,1)}) %all-gather.11.cloned.1.call-update) | async-done | bytes 1835024 | tf_op jit(solution)/shard_map/all_gather | solution.py:38
  429.8 10.7 %convolution_add_fusion = f32[512,2048]{1,0:T(8,128)} fusion(f32[512,2048]{1,0:T(8,128)} %fusion.17, bf16[512,1792]{1,0:T(8,128)(2,1)} %all-gather.11.cloned.1.call-done, bf16[1792,2048]{1,0:T(8,128)(2,1)} %param.9), kind=kOutput, calls=%fused_computation.9 | convolution fusion | flops 3759144960 | bytes 17563648 | tf_op jit(solution)/shard_map/dot_general | solution.py:55
  440.6 1.5 copy.13
  442.0 3.6 all-to-all-start
  445.7 25.6 %all-to-all-done = bf16[128,4,2048]{2,0,1:T(8,128)(2,1)S(1)} async-done(((bf16[128,4,2048]{2,0,1:T(8,128)(2,1)}), bf16[128,4,2048]{2,0,1:T(8,128)(2,1)S(1)}, u32[]{:S(2)}, u32[]{:S(2)}) %all-to-all-start) | async-done | bytes 2097184 | tf_op jit(solution)/shard_map/all_to_all | solution.py:40
  471.8 6.2 %psum.21 = f32[512]{0:T(512)S(1)} all-reduce(f32[512]{0:T(512)S(1)} %bitcast.25), channel_id=1, replica_groups=mesh['dp'=8,'tensor'=4] {'tensor'}, use_global_device_ids=true, to_apply=%region_1.0 | all-reduce | flops 512 | bytes 4096 | tf_op jit(solution)/shard_map/psum | solution.py:42
  478.1 2.5 multiply_convert_fusion.2
  480.6 6.1 %multiply_convert_fusion.1 = bf16[1792,2048]{1,0:T(8,128)(2,1)} fusion(bf16[512,1792]{1,0:T(8,128)(2,1)S(1)} %copy-done.2, bf16[512,2048]{1,0:T(8,128)(2,1)S(1)} %get-tuple-element.6), kind=kOutput, calls=%fused_computation.1 | convolution fusion | flops 3765436416 | bytes 11272192 | tf_op jit(solution)/shard_map/dot_general | solution.py:22
  486.7 6.1 %multiply_convert_fusion = bf16[1792,2048]{1,0:T(8,128)(2,1)} fusion(bf16[512,1792]{1,0:T(8,128)(2,1)S(1)} %copy-done.3, bf16[512,2048]{1,0:T(8,128)(2,1)S(1)} %get-tuple-element.6), kind=kOutput, calls=%fused_computation | convolution fusion | flops 3765436416 | bytes 11272192 | tf_op jit(solution)/shard_map/dot_general | solution.py:22
  492.8 35.9 %reduce-scatter.2.cloned.1.call-done = f32[64,2048]{1,0:T(8,128)} async-done(((f32[512,2048]{1,0:T(8,128)}), f32[64,2048]{1,0:T(8,128)}) %reduce-scatter.2.cloned.1.call-update) | async-done | bytes 524304 | tf_op jit(solution)/shard_map/reduce_scatter | solution.py:53
  528.7 1.4 fusion.16
  530.1 6.8 %psum.22 = f32[64]{0:T(128)S(1)} all-reduce(f32[64]{0:T(128)S(1)} %get-tuple-element.5), channel_id=1, replica_groups=mesh['dp'=8,'tensor'=4] {'tensor'}, use_global_device_ids=true, to_apply=%region_5.0 | all-reduce | flops 64 | bytes 512 | tf_op jit(solution)/shard_map/psum | solution.py:66
  537.0 20.4 %psum.23 = f32[2048]{0:T(1024)S(1)} all-reduce(f32[2048]{0:T(1024)S(1)} %get-tuple-element.4), channel_id=1, replica_groups=mesh['dp'=8,'tensor'=4] {'dp'}, use_global_device_ids=true, to_apply=%region_7.0 | all-reduce | flops 2048 | bytes 16384 | tf_op jit(solution)/shard_map/psum | solution.py:67
  557.4 0.6 broadcast_multiply_fusion
  558.0 2.1 fusion.12
  (24 shorter events, 1.8 us)
Async XLA Ops:
  7.2 183.1 %all-gather.7.cloned.1.call-start = ((), (), s32[]{:S(2)}) async-start(), calls=%async_computation.3 | async-start | bytes 36700160 | tf_op jit(solution)/shard_map/all_gather | solution.py:33
  7.9 1.6 copy-start
  7.9 182.4 %copy-start.1 = (f32[8192]{0:T(1024)S(1)}, f32[8192]{0:T(1024)}, u32[]{:S(2)}) copy-start(f32[8192]{0:T(1024)} %param.7) | copy-start | bytes 98308
  7.9 182.4 %copy-start.4 = (bf16[128,1792]{1,0:T(8,128)(2,1)S(1)}, bf16[128,1792]{1,0:T(8,128)(2,1)}, u32[]{:S(2)}) copy-start(bf16[128,1792]{1,0:T(8,128)(2,1)} %param.6) | copy-start | bytes 1376260
  7.9 362.0 %all-gather.5.cloned.1.call-start = ((), (), s32[]{:S(2)}) async-start(), calls=%async_computation.2 | async-start | bytes 36700160 | tf_op jit(solution)/shard_map/all_gather | solution.py:34
  8.7 398.0 %all-gather.9.cloned.1.call-start = ((), (), s32[]{:S(2)}) async-start(), calls=%async_computation.4 | async-start | bytes 2293760 | tf_op jit(solution)/shard_map/all_gather | solution.py:37
  385.4 44.4 %all-gather.11.cloned.1.call-start = ((), (), s32[]{:S(2)}) async-start(), calls=%async_computation.5 | async-start | bytes 2293760 | tf_op jit(solution)/shard_map/all_gather | solution.py:38
  386.0 142.7 %reduce-scatter.2.cloned.1.call-start = ((), (), s32[]{:S(2)}) async-start(), calls=%async_computation.6 | async-start | bytes 4718592 | tf_op jit(solution)/shard_map/reduce_scatter | solution.py:53
  442.0 29.3 %all-to-all-start = ((bf16[128,4,2048]{2,0,1:T(8,128)(2,1)}), bf16[128,4,2048]{2,0,1:T(8,128)(2,1)S(1)}, u32[]{:S(2)}, u32[]{:S(2)}) async-start(bf16[128,4,2048]{2,0,1:T(8,128)(2,1)} %bitcast.22), calls=%async_computation | async-start | bytes 4194304 | tf_op jit(solution)/shard_map/all_to_all | solution.py:40
  478.1 2.5 copy-start.2
  480.6 6.1 %copy-start.3 = (bf16[512,1792]{1,0:T(8,128)(2,1)S(1)}, bf16[512,1792]{1,0:T(8,128)(2,1)}, u32[]{:S(2)}) copy-start(bf16[512,1792]{1,0:T(8,128)(2,1)} %all-gather.11.cloned.1.call-done) | copy-start | bytes 5505028
Sparse Core Ops, SparseCore 0:
  9.6 180.6 all-gather.6
  191.9 177.9 all-gather.4
  385.5 21.1 all-gather.8
  408.7 21.1 all-gather.10
  440.7 87.9 reduce-scatter.1
where the time goes:
time: 567 us
  waiting for transfers between devices  440 us (78%)
  matrix products  65.8 us (12%)
  blocking collectives  33.5 us (6%)
  between operations  13.9 us (2%)
  other arithmetic  7.65 us (1%)
    all_gather x1, waiting for transfers between devices, shards(): lax.all_gather(gate_weight, 'tensor', axis=1, tiled=True)  180 us
    all_gather x1, waiting for transfers between devices, shards(): lax.all_gather(up_weight, 'tensor', axis=1, tiled=True)  162 us
    reduce_scatter x1, waiting for transfers between devices, shards(): lax.psum_scatter(jnp.dot(gate_all, gate_weight, preferred_element_type=jn...  35.9 us
    dot_general x2, matrix products, right_product(): lax.dot_general(left, weight, (((1,), (1,)), ((), ())), preferred_element...  33.3 us
    all_to_all x1, waiting for transfers between devices, shards(): lax.all_to_all(residual, 'tensor', split_axis=1, concat_axis=0, tiled=True)  25.6 us
    all_gather x1, waiting for transfers between devices, shards(): lax.all_gather(gate_delta, 'tensor', axis=0, tiled=True)  20.7 us
    psum x1, blocking collectives, shards(): gain_total = lax.psum(gain_part, 'dp')  20.4 us
    all_gather x1, waiting for transfers between devices, shards(): lax.all_gather(up_delta, 'tensor', axis=0, tiled=True)  13.5 us
  transfers between devices with their start and end apart: 6, of which 6 were waited for; matrix products, arithmetic and copies ran while one was open for 8% of the time, Pallas kernels for 0%

commit v1 on v0

v1 whole, which is shorter than its diff:
```python
import jax
import jax.numpy as jnp
from jax import lax
from jax.sharding import PartitionSpec as P


def activate(gate, up_proj, cotangent):
    cot_f = cotangent.astype(jnp.float32)
    sig = jax.nn.sigmoid(gate)
    gate_delta = (cot_f * up_proj * sig * (1.0 + gate * (1.0 - sig))).astype(jnp.bfloat16)
    up_delta = (cot_f * gate * sig).astype(jnp.bfloat16)
    return (gate_delta, up_delta)


def right_product(left, weight):
    return lax.dot_general(
        left, weight, (((1,), (1,)), ((), ())), preferred_element_type=jnp.float32
    )


def left_product(left, right):
    return lax.dot_general(
        left, right, (((0,), (0,)), ((), ())), preferred_element_type=jnp.float32
    )


def scattered_sum(part, axis):
    n = lax.axis_size(axis)
    pieces = part.astype(jnp.bfloat16).reshape(n, part.shape[0] // n, part.shape[1])
    pieces = lax.all_to_all(pieces, axis, split_axis=0, concat_axis=0, tiled=True)
    return jnp.sum(pieces.astype(jnp.float32), axis=0)


def shards(residual, hidden_cotangent, norm_gain, gate_weight, up_weight):
    width = residual.shape[1]
    slice_width = gate_weight.shape[1]
    tokens = residual.shape[0]
    feat_resid = lax.all_to_all(residual, "tensor", split_axis=1, concat_axis=0, tiled=True)
    resid_f = residual.astype(jnp.float32)
    own_inv = lax.rsqrt(jnp.mean(resid_f * resid_f, axis=-1) + 1e-05)
    feat_inv = lax.all_gather(own_inv, "tensor", axis=0, tiled=True)[:, None]
    feat_f = feat_resid.astype(jnp.float32)
    gain_slice = lax.dynamic_slice_in_dim(
        norm_gain, lax.axis_index("tensor") * slice_width, slice_width
    )
    feat_normed = (feat_f * feat_inv * gain_slice).astype(jnp.bfloat16)
    gate = scattered_sum(right_product(feat_normed, gate_weight), "tensor")
    up_proj = scattered_sum(right_product(feat_normed, up_weight), "tensor")
    gate_delta, up_delta = activate(gate, up_proj, hidden_cotangent)
    gate_all, up_all = (
        lax.all_gather(gate_delta, "tensor", axis=0, tiled=True),
        lax.all_gather(up_delta, "tensor", axis=0, tiled=True),
    )
    tokens_total = tokens * lax.axis_size("tensor")
    scale = tokens_total ** (-0.5)
    rows_each = tokens_total // lax.axis_size("dp")
    delta_part = jnp.dot(gate_all, gate_weight, preferred_element_type=jnp.float32) + jnp.dot(
        up_all, up_weight, preferred_element_type=jnp.float32
    )
    delta_rows = scattered_sum(delta_part, "dp")
    gate_grad = (left_product(gate_all, feat_normed) * scale).astype(jnp.bfloat16)
    up_grad = (left_product(up_all, feat_normed) * scale).astype(jnp.bfloat16)
    delta_f = delta_rows.astype(jnp.bfloat16).astype(jnp.float32)
    row_start = lax.axis_index("dp") * rows_each
    resid_rows = lax.dynamic_slice_in_dim(feat_resid, row_start, rows_each, 0).astype(jnp.float32)
    inv_rows = lax.dynamic_slice_in_dim(feat_inv, row_start, rows_each, 0)
    gain_part = jnp.sum(delta_f * resid_rows * inv_rows, axis=0)
    coeff_part = jnp.sum(gain_slice * delta_f * resid_rows, axis=1)
    coeff = lax.psum(coeff_part, "tensor")[:, None] / width
    gain_total = lax.psum(gain_part, "dp")
    input_grad = (
        inv_rows * gain_slice * delta_f - resid_rows * (inv_rows * inv_rows * inv_rows) * coeff
    )
    return (input_grad.astype(jnp.bfloat16), gate_grad, up_grad, gain_total * scale)


def solution(mesh):
    return jax.shard_map(
        shards,
        mesh=mesh,
        in_specs=(P("tensor", None), P("tensor", "dp"), P(), P("dp", "tensor"), P("dp", "tensor")),
        out_specs=(P("dp", "tensor"), P("dp", "tensor"), P("dp", "tensor"), P("tensor")),
        check_vma=False,
    )
```

time: 567 us -> 255 us (0.45)
  waiting for transfers between devices: 440 us -> 104 us
  blocking collectives: 33.5 us -> 49.4 us
  starting transfers between devices: 3.8 us -> 18.8 us
  matrix products: 65.8 us -> 53 us
    all_gather x2 -> x0, waiting for transfers between devices: 342 us -> none  [the longest x1 180 us: shards(): lax.all_gather(gate_weight, 'tensor', axis=1, tiled=True)]
    all_to_all x0 -> x3, waiting for transfers between devices: none -> 68.2 us  [scattered_sum(): lax.all_to_all(pieces, axis, split_axis=0, concat_axis=0, tiled=True)]
    reduce_scatter x1 -> x0, waiting for transfers between devices: 35.9 us -> none  [shards(): lax.psum_scatter(jnp.dot(gate_all, gate_weight, preferred_element_type=jn...]
    all_to_all x1, waiting for transfers between devices: 25.6 us -> 0.01 us  [shards(): lax.all_to_all(residual, 'tensor', split_axis=1, concat_axis=0, tiled=True)]
    all_gather x0 -> x1, blocking collectives: none -> 23.8 us  [shards(): feat_inv = lax.all_gather(own_inv, 'tensor', axis=0, tiled=True)[:, None]]
    dot_general x2, matrix products: 33.3 us -> 18 us  [right_product(): lax.dot_general(left, weight, (((1,), (1,)), ((), ())), preferred_element...]
    all_to_all x0 -> x3, starting transfers between devices: none -> 14.3 us  [scattered_sum(): lax.all_to_all(pieces, axis, split_axis=0, concat_axis=0, tiled=True)]
    reduce_sum x2 -> x4, other arithmetic: 0.97 us -> 7.8 us  [the longest x3 5.72 us: scattered_sum(): return jnp.sum(pieces.astype(jnp.float32), axis=0)]
  transfers between devices with their start and end apart: 6 -> 6, of which waited for: 6 -> 5; matrix products, arithmetic and copies ran while one was open for 8% -> 15% of each run, Pallas kernels for 0% -> 0%
where the time goes in v1:
time: 255 us; the launch traced here: 254 us
  waiting for transfers between devices  104 us (41%)
  matrix products  53 us (21%)
  blocking collectives  49.4 us (19%)
  starting transfers between devices  18.8 us (7%)
  between operations  14.1 us (6%)
  other arithmetic  11.6 us (5%)
  local copies, waits for them, and re-layouts  3.88 us (2%)
    all_to_all x3, waiting for transfers between devices, scattered_sum(): lax.all_to_all(pieces, axis, split_axis=0, concat_axis=0, tiled=True)  68.2 us
    all_gather x1, blocking collectives, shards(): feat_inv = lax.all_gather(own_inv, 'tensor', axis=0, tiled=True)[:, None]  23.8 us
    all_gather x1, waiting for transfers between devices, shards(): lax.all_gather(gate_delta, 'tensor', axis=0, tiled=True)  21.7 us
    psum x1, blocking collectives, shards(): gain_total = lax.psum(gain_part, 'dp')  19.7 us
    dot_general x2, matrix products, right_product(): lax.dot_general(left, weight, (((1,), (1,)), ((), ())), preferred_element...  18 us
    dot_general x2, matrix products, left_product(): lax.dot_general(left, right, (((0,), (0,)), ((), ())), preferred_element_...  15.4 us
    all_to_all x3, starting transfers between devices, scattered_sum(): lax.all_to_all(pieces, axis, split_axis=0, concat_axis=0, tiled=True)  14.3 us
    all_gather x1, waiting for transfers between devices, shards(): lax.all_gather(up_delta, 'tensor', axis=0, tiled=True)  13.1 us
  transfers between devices with their start and end apart: 6, of which 5 were waited for; matrix products, arithmetic and copies ran while one was open for 15% of the time, Pallas kernels for 0%

profile of v1, /device:TPU:0, one launch (start us, length us, event | category | flops | bytes accessed | tf_op | source)
XLA Modules:
  0.0 254.4 jit_solution(13967368267179482517)
XLA Ops:
  7.2 3.2 %copy.13 = bf16[16,4,8,2048]{3,2,0,1:T(8,128)(2,1)} copy(bf16[16,4,8,2048]{3,2,1,0:T(8,128)(2,1)} %bitcast.28) | data formatting | bytes 4194304 | tf_op jit(solution)/shard_map/all_to_all | solution.py:38
  10.3 4.2 %all-to-all-start = ((bf16[128,4,2048]{2,0,1:T(8,128)(2,1)}), bf16[128,4,2048]{2,0,1:T(8,128)(2,1)S(1)}, u32[]{:S(2)}, u32[]{:S(2)}) async-start(bf16[128,4,2048]{2,0,1:T(8,128)(2,1)} %bitcast.29), calls=%async_computation | async-start | bytes 4194304 | tf_op jit(solution)/shard_map/all_to_all | solution.py:38
  15.2 2.1 multiply_reduce_fusion
  17.3 23.8 %all-gather = f32[4,1,128]{2,1,0:T(1,128)S(1)} all-gather(f32[1,1,128]{2,1,0:T(1,128)S(1)} %rsqrt_bitcast_fusion), channel_id=1, replica_groups=mesh['dp'=8,'tensor'=4] {'tensor'}, dimensions={0}, use_global_device_ids=true | all-gather | bytes 2560 | tf_op jit(solution)/shard_map/all_gather | solution.py:41
  41.7 9.0 %convolution_convert_fusion = bf16[512,1792]{1,0:T(8,128)(2,1)} fusion(bf16[512,2048]{1,0:T(8,128)(2,1)S(1)} %multiply_convert_fusion.2, bf16[1792,2048]{1,0:T(8,128)(2,1)} %param.8), kind=kOutput, calls=%fused_computation.7 | convolution fusion | flops 3759013888 | bytes 11272192 | tf_op jit(solution)/shard_map/dot_general | solution.py:16
  50.7 4.4 %all-to-all-start.2 = ((bf16[4,128,1792]{2,1,0:T(8,128)(2,1)}), bf16[4,128,1792]{2,1,0:T(8,128)(2,1)}, u32[]{:S(2)}, u32[]{:S(2)}) async-start(bf16[4,128,1792]{2,1,0:T(8,128)(2,1)} %bitcast.32), calls=%async_computation.2 | async-start | bytes 3670016 | tf_op jit(solution)/shard_map/all_to_all | solution.py:30
  55.1 9.0 %convolution_convert_fusion.1 = bf16[512,1792]{1,0:T(8,128)(2,1)} fusion(bf16[512,2048]{1,0:T(8,128)(2,1)} %copy-done, bf16[1792,2048]{1,0:T(8,128)(2,1)} %param.9), kind=kOutput, calls=%fused_computation.8 | convolution fusion | flops 3759013888 | bytes 11272192 | tf_op jit(solution)/shard_map/dot_general | solution.py:16
  64.1 14.0 %all-to-all-done.2 = bf16[4,128,1792]{2,1,0:T(8,128)(2,1)} async-done(((bf16[4,128,1792]{2,1,0:T(8,128)(2,1)}), bf16[4,128,1792]{2,1,0:T(8,128)(2,1)}, u32[]{:S(2)}, u32[]{:S(2)}) %all-to-all-start.2) | async-done | bytes 1835040 | tf_op jit(solution)/shard_map/all_to_all | solution.py:30
  78.0 4.4 %all-to-all-start.1 = ((bf16[4,128,1792]{2,1,0:T(8,128)(2,1)}), bf16[4,128,1792]{2,1,0:T(8,128)(2,1)}, u32[]{:S(2)}, u32[]{:S(2)}) async-start(bf16[4,128,1792]{2,1,0:T(8,128)(2,1)} %bitcast.31), calls=%async_computation.1 | async-start | bytes 3670016 | tf_op jit(solution)/shard_map/all_to_all | solution.py:30
  82.5 1.9 convert_reduce_fusion
  84.4 21.0 %all-to-all-done.1 = bf16[4,128,1792]{2,1,0:T(8,128)(2,1)} async-done(((bf16[4,128,1792]{2,1,0:T(8,128)(2,1)}), bf16[4,128,1792]{2,1,0:T(8,128)(2,1)}, u32[]{:S(2)}, u32[]{:S(2)}) %all-to-all-start.1) | async-done | bytes 1835040 | tf_op jit(solution)/shard_map/all_to_all | solution.py:30
  105.4 1.9 convert_reduce_fusion.1
  107.3 1.4 fusion.4
  109.4 21.7 %all-gather.4.cloned.1.call-done = bf16[512,1792]{1,0:T(8,128)(2,1)} async-done(((bf16[128,1792]{1,0:T(8,128)(2,1)}), bf16[512,1792]{1,0:T(8,128)(2,1)}) %all-gather.4.cloned.1.call-update) | async-done | bytes 1835024 | tf_op jit(solution)/shard_map/all_gather | solution.py:51
  131.1 9.6 %fusion.11 = f32[512,2048]{1,0:T(8,128)} fusion(bf16[512,1792]{1,0:T(8,128)(2,1)} %all-gather.4.cloned.1.call-done, bf16[1792,2048]{1,0:T(8,128)(2,1)} %param.8), kind=kOutput, calls=%fused_computation.33 | convolution fusion | flops 3758096384 | bytes 13369344 | tf_op jit(solution)/shard_map/dot_general | solution.py:57
  140.7 13.1 %all-gather.6.cloned.1.call-done = bf16[512,1792]{1,0:T(8,128)(2,1)} async-done(((bf16[128,1792]{1,0:T(8,128)(2,1)}), bf16[512,1792]{1,0:T(8,128)(2,1)}) %all-gather.6.cloned.1.call-update) | async-done | bytes 1835024 | tf_op jit(solution)/shard_map/all_gather | solution.py:52
  153.8 10.0 %add_convert_fusion = bf16[512,2048]{1,0:T(8,128)(2,1)} fusion(f32[512,2048]{1,0:T(8,128)} %fusion.11, bf16[512,1792]{1,0:T(8,128)(2,1)} %all-gather.6.cloned.1.call-done, bf16[1792,2048]{1,0:T(8,128)(2,1)} %param.9), kind=kOutput, calls=%fused_computation.2 | convolution fusion | flops 3760193536 | bytes 15466496 | tf_op jit(solution)/shard_map/dot_general | solution.py:57
  163.8 5.5 %all-to-all-start.3 = ((bf16[8,64,2048]{2,1,0:T(8,128)(2,1)}), bf16[8,64,2048]{2,1,0:T(8,128)(2,1)}, u32[]{:S(2)}, u32[]{:S(2)}) async-start(bf16[8,64,2048]{2,1,0:T(8,128)(2,1)} %bitcast.30), calls=%async_computation.3 | async-start | bytes 4194304 | tf_op jit(solution)/shard_map/all_to_all | solution.py:30
  169.4 9.4 %multiply_convert_fusion = bf16[1792,2048]{1,0:T(8,128)(2,1)} fusion(bf16[512,1792]{1,0:T(8,128)(2,1)} %all-gather.6.cloned.1.call-done, bf16[512,2048]{1,0:T(8,128)(2,1)} %copy-done), kind=kOutput, calls=%fused_computation | convolution fusion | flops 3765436416 | bytes 11272192 | tf_op jit(solution)/shard_map/dot_general | solution.py:22
  178.8 6.1 %multiply_convert_fusion.1 = bf16[1792,2048]{1,0:T(8,128)(2,1)} fusion(bf16[512,1792]{1,0:T(8,128)(2,1)S(1)} %copy-done.3, bf16[512,2048]{1,0:T(8,128)(2,1)S(1)} %copy-done.1), kind=kOutput, calls=%fused_computation.1 | convolution fusion | flops 3765436416 | bytes 11272192 | tf_op jit(solution)/shard_map/dot_general | solution.py:22
  184.9 33.2 %all-to-all-done.3 = bf16[8,64,2048]{2,1,0:T(8,128)(2,1)} async-done(((bf16[8,64,2048]{2,1,0:T(8,128)(2,1)}), bf16[8,64,2048]{2,1,0:T(8,128)(2,1)}, u32[]{:S(2)}, u32[]{:S(2)}) %all-to-all-start.3) | async-done | bytes 2097184 | tf_op jit(solution)/shard_map/all_to_all | solution.py:30
  218.1 2.0 reduce_sum.60
  220.3 19.7 %psum.15 = f32[2048]{0:T(1024)S(1)} all-reduce(f32[2048]{0:T(1024)S(1)} %get-tuple-element.4), channel_id=1, replica_groups=mesh['dp'=8,'tensor'=4] {'dp'}, use_global_device_ids=true, to_apply=%region_7.0 | all-reduce | flops 2048 | bytes 16384 | tf_op jit(solution)/shard_map/psum | solution.py:70
  240.6 5.9 %psum.14 = f32[64]{0:T(128)S(1)} all-reduce(f32[64]{0:T(128)S(1)} %get-tuple-element.5), channel_id=1, replica_groups=mesh['dp'=8,'tensor'=4] {'tensor'}, use_global_device_ids=true, to_apply=%region_5.0 | all-reduce | flops 64 | bytes 512 | tf_op jit(solution)/shard_map/psum | solution.py:69
  (21 shorter events, 3.9 us)
Async XLA Ops:
  10.3 30.8 %all-to-all-start = ((bf16[128,4,2048]{2,0,1:T(8,128)(2,1)}), bf16[128,4,2048]{2,0,1:T(8,128)(2,1)S(1)}, u32[]{:S(2)}, u32[]{:S(2)}) async-start(bf16[128,4,2048]{2,0,1:T(8,128)(2,1)} %bitcast.29), calls=%async_computation | async-start | bytes 4194304 | tf_op jit(solution)/shard_map/all_to_all | solution.py:38
  41.7 9.0 %copy-start = (bf16[512,2048]{1,0:T(8,128)(2,1)}, bf16[512,2048]{1,0:T(8,128)(2,1)S(1)}, u32[]{:S(2)}) copy-start(bf16[512,2048]{1,0:T(8,128)(2,1)S(1)} %multiply_convert_fusion.2) | copy-start | bytes 6291460
  50.7 27.4 %all-to-all-start.2 = ((bf16[4,128,1792]{2,1,0:T(8,128)(2,1)}), bf16[4,128,1792]{2,1,0:T(8,128)(2,1)}, u32[]{:S(2)}, u32[]{:S(2)}) async-start(bf16[4,128,1792]{2,1,0:T(8,128)(2,1)} %bitcast.32), calls=%async_computation.2 | async-start | bytes 3670016 | tf_op jit(solution)/shard_map/all_to_all | solution.py:30
  78.0 27.4 %all-to-all-start.1 = ((bf16[4,128,1792]{2,1,0:T(8,128)(2,1)}), bf16[4,128,1792]{2,1,0:T(8,128)(2,1)}, u32[]{:S(2)}, u32[]{:S(2)}) async-start(bf16[4,128,1792]{2,1,0:T(8,128)(2,1)} %bitcast.31), calls=%async_computation.1 | async-start | bytes 3670016 | tf_op jit(solution)/shard_map/all_to_all | solution.py:30
  82.4 24.8 %copy-start.2 = (bf16[128,1792]{1,0:T(8,128)(2,1)S(1)}, bf16[128,1792]{1,0:T(8,128)(2,1)}, u32[]{:S(2)}) copy-start(bf16[128,1792]{1,0:T(8,128)(2,1)} %param.6) | copy-start | bytes 1376260
  82.4 48.6 %all-gather.4.cloned.1.call-start = ((), (), s32[]{:S(2)}) async-start(), calls=%async_computation.4 | async-start | bytes 2293760 | tf_op jit(solution)/shard_map/all_gather | solution.py:51
  108.7 45.1 %all-gather.6.cloned.1.call-start = ((), (), s32[]{:S(2)}) async-start(), calls=%async_computation.5 | async-start | bytes 2293760 | tf_op jit(solution)/shard_map/all_gather | solution.py:52
  163.8 54.3 %all-to-all-start.3 = ((bf16[8,64,2048]{2,1,0:T(8,128)(2,1)}), bf16[8,64,2048]{2,1,0:T(8,128)(2,1)}, u32[]{:S(2)}, u32[]{:S(2)}) async-start(bf16[8,64,2048]{2,1,0:T(8,128)(2,1)} %bitcast.30), calls=%async_computation.3 | async-start | bytes 4194304 | tf_op jit(solution)/shard_map/all_to_all | solution.py:30
  169.4 9.4 %copy-start.1 = (bf16[512,2048]{1,0:T(8,128)(2,1)S(1)}, bf16[512,2048]{1,0:T(8,128)(2,1)}, u32[]{:S(2)}) copy-start(bf16[512,2048]{1,0:T(8,128)(2,1)} %copy-done) | copy-start | bytes 6291460
  169.4 9.4 %copy-start.3 = (bf16[512,1792]{1,0:T(8,128)(2,1)S(1)}, bf16[512,1792]{1,0:T(8,128)(2,1)}, u32[]{:S(2)}) copy-start(bf16[512,1792]{1,0:T(8,128)(2,1)} %all-gather.4.cloned.1.call-done) | copy-start | bytes 5505028
Sparse Core Ops, SparseCore 0:
  108.8 22.2 all-gather.3
  132.6 21.1 all-gather.5

commit v2 on v1

--- a/solution.py
+++ b/solution.py
@@ -1,6 +1,10 @@
+import functools
+
 import jax
 import jax.numpy as jnp
 from jax import lax
+from jax.experimental import pallas as pl
+from jax.experimental.pallas import tpu as pltpu
 from jax.sharding import PartitionSpec as P
 
 
@@ -29,6 +33,185 @@
     pieces = part.astype(jnp.bfloat16).reshape(n, part.shape[0] // n, part.shape[1])
     pieces = lax.all_to_all(pieces, axis, split_axis=0, concat_axis=0, tiled=True)
     return jnp.sum(pieces.astype(jnp.float32), axis=0)
+
+
+MESH = pl.DeviceIdType.MESH
+
+
+def delta_kernel(
+    groups, chunks, normed, cot, gate_w, up_w, gate_all, up_all,
+    paired, weights, pair_out, pair_in, own, far_out, far_in,
+    w_sem, pair_s, pair_r, far_s, far_r, peer_s, peer_r, sib_s, sib_r,
+):
+    me = lax.axis_index("tensor")
+    dp = lax.axis_index("dp")
+    core, group = lax.rem(me, 2), me // 2
+    sib_core = 1 - core
+    rows = cot.shape[0]
+    half = groups * rows
+    cols = cot.shape[1] // chunks
+    sibling = (dp, group * 2 + sib_core)
+
+    def other(j):
+        return lax.rem(group + j, groups)
+
+    def block(g, c):
+        return pl.ds(pl.multiple_of((g * 2 + c) * rows, rows), rows)
+
+    def span(k):
+        return pl.ds(0, cols) if chunks == 1 else pl.ds(pl.multiple_of(k * cols, cols), cols)
+
+    def w_copies(k):
+        start = pl.ds(pl.multiple_of(k * cols, cols), cols)
+        return [
+            pltpu.make_async_copy(w.at[start], weights.at[k, pl.ds(i * cols, cols)], w_sem.at[k, i])
+            for i, w in enumerate((gate_w, up_w))
+        ]
+
+    for k in range(chunks):
+        for copy in w_copies(k):
+            copy.start()
+
+    barrier = pltpu.get_barrier_semaphore()
+    pl.semaphore_signal(barrier, inc=1, device_id=sibling, device_id_type=MESH)
+    for j in range(1, groups):
+        pl.semaphore_signal(
+            barrier, inc=1, device_id=(dp, other(j) * 2 + core), device_id_type=MESH
+        )
+
+    for g in range(groups):
+        paired[pl.ds(g * rows, rows)] = normed[block(g, sib_core)]
+        paired[pl.ds(half + g * rows, rows)] = normed[block(g, core)]
+    pl.semaphore_wait(barrier, groups)
+
+    def pair_copy(k):
+        return pltpu.make_async_remote_copy(
+            pair_out.at[k], pair_in.at[k], pair_s.at[k], pair_r.at[k],
+            device_id=sibling, device_id_type=MESH,
+        )
+
+    def far_copy(k, j, source):
+        return pltpu.make_async_remote_copy(
+            far_out.at[k, j - 1], far_in.at[k, source], far_s.at[k, j - 1], far_r.at[k, source],
+            device_id=(dp, other(j) * 2 + core), device_id_type=MESH,
+        )
+
+    def peer_copy(k, j, source, i):
+        part = (gate_all, up_all)[i].at[block(source, core), span(k)]
+        return pltpu.make_async_remote_copy(
+            part, part, peer_s.at[k, j - 1, i], peer_r.at[k, source, i],
+            device_id=(dp, other(j) * 2 + core), device_id_type=MESH,
+        )
+
+    def sib_copy(k, source, i, c):
+        part = (gate_all, up_all)[i].at[block(source, c), span(k)]
+        return pltpu.make_async_remote_copy(
+            part, part, sib_s.at[k, source, i], sib_r.at[k, source, i],
+            device_id=sibling, device_id_type=MESH,
+        )
+
+    def product(k):
+        for copy in w_copies(k):
+            copy.wait()
+        part = right_product(paired[...], weights[k])
+        pair_out[k] = part[:half].astype(jnp.bfloat16)
+        own[k] = part[half:]
+        pair_copy(k).start()
+
+    def pair_sum(k):
+        pair_copy(k).wait_recv()
+        for j in range(1, groups):
+            at = pl.ds(pl.multiple_of(other(j) * rows, rows), rows)
+            total = own[k, at] + pair_in[k, at].astype(jnp.float32)
+            far_out[k, j - 1] = total.astype(jnp.bfloat16)
+            far_copy(k, j, group).start()
+
+    def deltas(k):
+        at = pl.ds(pl.multiple_of(group * rows, rows), rows)
+        total = own[k, at] + pair_in[k, at].astype(jnp.float32)
+        for j in range(1, groups):
+            far_copy(k, j, other(j)).wait_recv()
+            total += far_in[k, other(j)].astype(jnp.float32)
+        gate_d, up_d = activate(total[:, :cols], total[:, cols:], cot[:, span(k)])
+        gate_all[block(group, core), span(k)] = gate_d
+        up_all[block(group, core), span(k)] = up_d
+        for i in range(2):
+            for j in range(1, groups):
+                peer_copy(k, j, group, i).start()
+            sib_copy(k, group, i, core).start()
+
+    def forward(k):
+        for j in range(1, groups):
+            for i in range(2):
+                peer_copy(k, j, other(j), i).wait_recv()
+                sib_copy(k, other(j), i, core).start()
+
+    stages = ((product, 0), (pair_sum, 1), (deltas, 3), (forward, 5))
+
+    def step(s, carry):
+        for stage, lag in stages:
+            @pl.when((s >= lag) & (s < chunks + lag))
+            def _():
+                stage(s - lag)
+        return carry
+
+    lax.fori_loop(0, chunks + stages[-1][1], step, 0)
+
+    def finish(k, carry):
+        pair_copy(k).wait_send()
+        for j in range(1, groups):
+            far_copy(k, j, group).wait_send()
+            for i in range(2):
+                peer_copy(k, j, group, i).wait_send()
+        for g in range(groups):
+            for i in range(2):
+                sib_copy(k, g, i, core).wait_send()
+                sib_copy(k, g, i, sib_core).wait_recv()
+        return carry
+
+    lax.fori_loop(0, chunks, finish, 0)
+
+
+def all_deltas(normed, cot, gate_weight, up_weight):
+    rows, hidden = cot.shape
+    total, width = normed.shape
+    groups = total // rows // 2
+    chunks = hidden // 256 if hidden % 256 == 0 else 1
+    cols = hidden // chunks
+    half = groups * rows
+    dma = pltpu.SemaphoreType.DMA
+    vmem = pl.BlockSpec(memory_space=pltpu.VMEM)
+    flops = 4 * total * width * hidden
+    return pl.pallas_call(
+        functools.partial(delta_kernel, groups, chunks),
+        out_shape=[jax.ShapeDtypeStruct((total, hidden), jnp.bfloat16)] * 2,
+        in_specs=[vmem, vmem, pl.BlockSpec(memory_space=pl.ANY), pl.BlockSpec(memory_space=pl.ANY)],
+        out_specs=[vmem, vmem],
+        scratch_shapes=[
+            pltpu.VMEM((total, width), jnp.bfloat16),
+            pltpu.VMEM((chunks, 2 * cols, width), jnp.bfloat16),
+            pltpu.VMEM((chunks, half, 2 * cols), jnp.bfloat16),
+            pltpu.VMEM((chunks, half, 2 * cols), jnp.bfloat16),
+            pltpu.VMEM((chunks, half, 2 * cols), jnp.float32),
+            pltpu.VMEM((chunks, max(groups - 1, 1), rows, 2 * cols), jnp.bfloat16),
+            pltpu.VMEM((chunks, groups, rows, 2 * cols), jnp.bfloat16),
+            dma((chunks, 2)),
+            dma((chunks,)),
+            dma((chunks,)),
+            dma((chunks, groups)),
+            dma((chunks, groups)),
+            dma((chunks, groups, 2)),
+            dma((chunks, groups, 2)),
+            dma((chunks, groups, 2)),
+            dma((chunks, groups, 2)),
+        ],
+        compiler_params=pltpu.CompilerParams(
+            collective_id=0, has_side_effects=True, vmem_limit_bytes=56 * 1024 * 1024
+        ),
+        cost_estimate=pl.CostEstimate(
+            flops=flops, bytes_accessed=4 * hidden * width, transcendentals=0
+        ),
+    )(normed, cot, gate_weight, up_weight)
 
 
 def shards(residual, hidden_cotangent, norm_gain, gate_weight, up_weight):
@@ -44,13 +227,7 @@
         norm_gain, lax.axis_index("tensor") * slice_width, slice_width
     )
     feat_normed = (feat_f * feat_inv * gain_slice).astype(jnp.bfloat16)
-    gate = scattered_sum(right_product(feat_normed, gate_weight), "tensor")
-    up_proj = scattered_sum(right_product(feat_normed, up_weight), "tensor")
-    gate_delta, up_delta = activate(gate, up_proj, hidden_cotangent)
-    gate_all, up_all = (
-        lax.all_gather(gate_delta, "tensor", axis=0, tiled=True),
-        lax.all_gather(up_delta, "tensor", axis=0, tiled=True),
-    )
+    gate_all, up_all = all_deltas(feat_normed, hidden_cotangent, gate_weight, up_weight)
     tokens_total = tokens * lax.axis_size("tensor")
     scale = tokens_total ** (-0.5)
     rows_each = tokens_total // lax.axis_size("dp")

time: 255 us -> 188 us (0.74)
  waiting for transfers between devices: 104 us -> 33.3 us
  Pallas kernels: 0 us -> 50.9 us
  matrix products: 53 us -> 30.8 us
  between operations: 14.1 us -> 0.69 us
  starting transfers between devices: 18.8 us -> 10.9 us
  other arithmetic: 11.6 us -> 7.79 us
    pallas_call x0 -> x1, Pallas kernels: none -> 50.9 us  [all_deltas(): pl.pallas_call(functools.partial(delta_kernel, groups, chunks), out_shape...]
    all_to_all x3 -> x1, waiting for transfers between devices: 68.2 us -> 33.3 us  [scattered_sum(): lax.all_to_all(pieces, axis, split_axis=0, concat_axis=0, tiled=True)]
    all_gather x2 -> x0, waiting for transfers between devices: 34.8 us -> none  [the longest x1 21.7 us: shards(): lax.all_gather(gate_delta, 'tensor', axis=0, tiled=True)]
    dot_general x2 -> x0, matrix products: 18 us -> none  [right_product(): lax.dot_general(left, weight, (((1,), (1,)), ((), ())), preferred_element...]
    all_to_all x3 -> x1, starting transfers between devices: 14.3 us -> 6.65 us  [scattered_sum(): lax.all_to_all(pieces, axis, split_axis=0, concat_axis=0, tiled=True)]
    reduce_sum x3 -> x1, other arithmetic: 5.72 us -> 1.96 us  [scattered_sum(): return jnp.sum(pieces.astype(jnp.float32), axis=0)]
    dot_general x1, matrix products: 9.61 us -> 6.9 us  [shards(): jnp.dot(gate_all, gate_weight, preferred_element_type=jnp.float32)]
  transfers between devices with their start and end apart: 6 -> 2, of which waited for: 5 -> 1; matrix products, arithmetic and copies ran while one was open for 15% -> 10% of each run, Pallas kernels for 0% -> 0%
where the time goes in v2:
time: 188 us; the launch traced here: 187 us
  Pallas kernels  50.9 us (27%)
  blocking collectives  49.2 us (26%)
  waiting for transfers between devices  33.3 us (18%)
  matrix products  30.8 us (16%)
  starting transfers between devices  10.9 us (6%)
  other arithmetic  7.79 us (4%)
  local copies, waits for them, and re-layouts  3.87 us (2%)
    pallas_call x1, Pallas kernels, all_deltas(): pl.pallas_call(functools.partial(delta_kernel, groups, chunks), out_shape...  50.9 us
    all_to_all x1, waiting for transfers between devices, scattered_sum(): lax.all_to_all(pieces, axis, split_axis=0, concat_axis=0, tiled=True)  33.3 us
    all_gather x1, blocking collectives, shards(): feat_inv = lax.all_gather(own_inv, 'tensor', axis=0, tiled=True)[:, None]  23.8 us
    psum x1, blocking collectives, shards(): gain_total = lax.psum(gain_part, 'dp')  19.7 us
    dot_general x2, matrix products, left_product(): lax.dot_general(left, right, (((0,), (0,)), ((), ())), preferred_element_...  15.4 us
    dot_general x1, matrix products, shards(): jnp.dot(up_all, up_weight, preferred_element_type=jnp.float32)  8.43 us
    dot_general x1, matrix products, shards(): jnp.dot(gate_all, gate_weight, preferred_element_type=jnp.float32)  6.9 us
    all_to_all x1, starting transfers between devices, scattered_sum(): lax.all_to_all(pieces, axis, split_axis=0, concat_axis=0, tiled=True)  6.65 us
  transfers between devices with their start and end apart: 2, of which 1 were waited for; matrix products, arithmetic and copies ran while one was open for 10% of the time, Pallas kernels for 0%

profile of v2, /device:TPU:0, one launch (start us, length us, event | category | flops | bytes accessed | tf_op | source)
XLA Modules:
  0.0 187.4 jit_solution(8024760501545201166)
XLA Ops:
  0.6 3.2 %copy.13 = bf16[16,4,8,2048]{3,2,0,1:T(8,128)(2,1)} copy(bf16[16,4,8,2048]{3,2,1,0:T(8,128)(2,1)} %bitcast.22) | data formatting | bytes 4194304 | tf_op jit(solution)/shard_map/all_to_all | solution.py:221
  3.8 4.2 %all-to-all-start = ((bf16[128,4,2048]{2,0,1:T(8,128)(2,1)}), bf16[128,4,2048]{2,0,1:T(8,128)(2,1)S(1)}, u32[]{:S(2)}, u32[]{:S(2)}) async-start(bf16[128,4,2048]{2,0,1:T(8,128)(2,1)} %bitcast.23), calls=%async_computation | async-start | bytes 4194304 | tf_op jit(solution)/shard_map/all_to_all | solution.py:221
  8.0 0.7 dynamic_slice.7
  8.7 2.1 %multiply_reduce_fusion = f32[128]{0:T(128)S(1)} fusion(bf16[128,8192]{1,0:T(8,128)(2,1)} %param.5), kind=kLoop, calls=%fused_computation.4 | loop fusion | flops 3145600 | bytes 2097664 | tf_op jit(solution)/shard_map/reduce_sum | solution.py:223
  10.8 23.8 %all-gather = f32[4,1,128]{2,1,0:T(1,128)S(1)} all-gather(f32[1,1,128]{2,1,0:T(1,128)S(1)} %rsqrt_bitcast_fusion), channel_id=1, replica_groups=mesh['dp'=8,'tensor'=4] {'tensor'}, dimensions={0}, use_global_device_ids=true | all-gather | bytes 2560 | tf_op jit(solution)/shard_map/all_gather | solution.py:224
  34.6 0.0 all-to-all-done
  34.6 1.9 multiply_convert_fusion.2.normed
  36.5 50.9 %shard_map.84 = (bf16[512,1792]{1,0:T(8,128)(2,1)}, bf16[512,1792]{1,0:T(8,128)(2,1)}) custom-call(bf16[512,2048]{1,0:T(8,128)(2,1)} %multiply_convert_fusion.2.normed, bf16[128,1792]{1,0:T(8,128)(2,1)} %cot.1, bf16[1792,2048]{1,0:T(8,128)(2,1)} %gate_w.1, bf16[1792,2048]{1,0:T(8,128)(2,1)} %up_w.1), custom_call_target="tpu_custom_call" | custom-call | flops 7516192768 | bytes 14680064 | tf_op jit(solution)/shard_map/pallas_call | solution.py:185
  87.4 0.0 copy-start.2
  87.4 6.9 %fusion.6 = f32[512,2048]{1,0:T(8,128)S(1)} fusion(bf16[512,1792]{1,0:T(8,128)(2,1)} %get-tuple-element.6, bf16[1792,2048]{1,0:T(8,128)(2,1)} %gate_w.1), kind=kOutput, calls=%fused_computation.21 | convolution fusion | flops 3758096384 | bytes 13369344 | tf_op jit(solution)/shard_map/dot_general | solution.py:234
  94.3 0.0 copy-done.2
  94.3 8.4 %add_convert_fusion = bf16[512,2048]{1,0:T(8,128)(2,1)} fusion(f32[512,2048]{1,0:T(8,128)S(1)} %fusion.6, bf16[512,1792]{1,0:T(8,128)(2,1)S(1)} %copy-done.2, bf16[1792,2048]{1,0:T(8,128)(2,1)} %up_w.1), kind=kOutput, calls=%fused_computation.2 | convolution fusion | flops 3760193536 | bytes 15466496 | tf_op jit(solution)/shard_map/dot_general | solution.py:234
  102.8 6.7 %all-to-all-start.1 = ((bf16[8,64,2048]{2,1,0:T(8,128)(2,1)}), bf16[8,64,2048]{2,1,0:T(8,128)(2,1)}, u32[]{:S(2)}, u32[]{:S(2)}) async-start(bf16[8,64,2048]{2,1,0:T(8,128)(2,1)} %bitcast.24), calls=%async_computation.1 | async-start | bytes 4194304 | tf_op jit(solution)/shard_map/all_to_all | solution.py:34
  109.4 0.1 multiply_multiply_fusion
  109.5 9.4 %multiply_convert_fusion = bf16[1792,2048]{1,0:T(8,128)(2,1)} fusion(bf16[512,1792]{1,0:T(8,128)(2,1)} %get-tuple-element.7, bf16[512,2048]{1,0:T(8,128)(2,1)} %multiply_convert_fusion.2.normed), kind=kOutput, calls=%fused_computation | convolution fusion | flops 3765436416 | bytes 11272192 | tf_op jit(solution)/shard_map/dot_general | solution.py:26
  118.8 0.0 copy-done
  118.9 6.1 %multiply_convert_fusion.1 = bf16[1792,2048]{1,0:T(8,128)(2,1)} fusion(bf16[512,1792]{1,0:T(8,128)(2,1)S(1)} %copy-done.1, bf16[512,2048]{1,0:T(8,128)(2,1)S(1)} %copy-done), kind=kOutput, calls=%fused_computation.1 | convolution fusion | flops 3765436416 | bytes 11272192 | tf_op jit(solution)/shard_map/dot_general | solution.py:26
  124.9 33.3 %all-to-all-done.1 = bf16[8,64,2048]{2,1,0:T(8,128)(2,1)} async-done(((bf16[8,64,2048]{2,1,0:T(8,128)(2,1)}), bf16[8,64,2048]{2,1,0:T(8,128)(2,1)}, u32[]{:S(2)}, u32[]{:S(2)}) %all-to-all-start.1) | async-done | bytes 2097184 | tf_op jit(solution)/shard_map/all_to_all | solution.py:34
  158.3 2.0 %reduce_sum.40 = bf16[64,2048]{1,0:T(8,128)(2,1)S(1)} reduce(bf16[8,64,2048]{2,1,0:T(8,128)(2,1)} %all-to-all-done.1, bf16[]{:T(256)} %constant.31.clone.1), dimensions={0}, to_apply=%region_1.0 | reduce | flops 917504 | bytes 2359298 | tf_op jit(solution)/shard_map/reduce_sum | solution.py:35
  160.2 0.2 fusion.5
  160.5 19.7 %psum.15 = f32[2048]{0:T(1024)S(1)} all-reduce(f32[2048]{0:T(1024)S(1)} %get-tuple-element.8), channel_id=1, replica_groups=mesh['dp'=8,'tensor'=4] {'dp'}, use_global_device_ids=true, to_apply=%region_5.0 | all-reduce | flops 2048 | bytes 16384 | tf_op jit(solution)/shard_map/psum | solution.py:247
  180.2 0.6 broadcast_multiply_fusion
  180.8 5.6 %psum.14 = f32[64]{0:T(128)S(1)} all-reduce(f32[64]{0:T(128)S(1)} %get-tuple-element.9), channel_id=1, replica_groups=mesh['dp'=8,'tensor'=4] {'tensor'}, use_global_device_ids=true, to_apply=%region_3.0 | all-reduce | flops 64 | bytes 512 | tf_op jit(solution)/shard_map/psum | solution.py:246
  186.4 1.0 fusion.1
  (5 shorter events, 0.0 us)
Async XLA Ops:
  3.8 30.8 %all-to-all-start = ((bf16[128,4,2048]{2,0,1:T(8,128)(2,1)}), bf16[128,4,2048]{2,0,1:T(8,128)(2,1)S(1)}, u32[]{:S(2)}, u32[]{:S(2)}) async-start(bf16[128,4,2048]{2,0,1:T(8,128)(2,1)} %bitcast.23), calls=%async_computation | async-start | bytes 4194304 | tf_op jit(solution)/shard_map/all_to_all | solution.py:221
  87.4 6.9 %copy-start.2 = (bf16[512,1792]{1,0:T(8,128)(2,1)S(1)}, bf16[512,1792]{1,0:T(8,128)(2,1)}, u32[]{:S(2)}) copy-start(bf16[512,1792]{1,0:T(8,128)(2,1)} %get-tuple-element.7) | copy-start | bytes 5505028
  102.8 55.5 %all-to-all-start.1 = ((bf16[8,64,2048]{2,1,0:T(8,128)(2,1)}), bf16[8,64,2048]{2,1,0:T(8,128)(2,1)}, u32[]{:S(2)}, u32[]{:S(2)}) async-start(bf16[8,64,2048]{2,1,0:T(8,128)(2,1)} %bitcast.24), calls=%async_computation.1 | async-start | bytes 4194304 | tf_op jit(solution)/shard_map/all_to_all | solution.py:34
  109.5 9.4 %copy-start = (bf16[512,2048]{1,0:T(8,128)(2,1)S(1)}, bf16[512,2048]{1,0:T(8,128)(2,1)}, u32[]{:S(2)}) copy-start(bf16[512,2048]{1,0:T(8,128)(2,1)} %multiply_convert_fusion.2.normed) | copy-start | bytes 6291460
  109.5 9.4 %copy-start.1 = (bf16[512,1792]{1,0:T(8,128)(2,1)S(1)}, bf16[512,1792]{1,0:T(8,128)(2,1)}, u32[]{:S(2)}) copy-start(bf16[512,1792]{1,0:T(8,128)(2,1)} %get-tuple-element.6) | copy-start | bytes 5505028

commit v3 on v2

--- a/solution.py
+++ b/solution.py
@@ -26,13 +26,6 @@
     return lax.dot_general(
         left, right, (((0,), (0,)), ((), ())), preferred_element_type=jnp.float32
     )
-
-
-def scattered_sum(part, axis):
-    n = lax.axis_size(axis)
-    pieces = part.astype(jnp.bfloat16).reshape(n, part.shape[0] // n, part.shape[1])
-    pieces = lax.all_to_all(pieces, axis, split_axis=0, concat_axis=0, tiled=True)
-    return jnp.sum(pieces.astype(jnp.float32), axis=0)
 
 
 MESH = pl.DeviceIdType.MESH
@@ -214,6 +207,215 @@
     )(normed, cot, gate_weight, up_weight)
 
 
+def input_kernel(
+    scale, gate_all, up_all, gate_w, up_w, resid, inv, gain, grad, gain_grad,
+    paired, weights, pair_out, pair_in, own, far_out, far_in, delta, gain_in, coeff_in,
+    w_sem, pair_s, pair_r, far_s, far_r, gain_s, gain_r, coeff_s, coeff_r,
+):
+    me = lax.axis_index("tensor")
+    dp = lax.axis_index("dp")
+    n_tensor, n_dp = coeff_in.shape[0], gain_in.shape[0]
+    chunks, _, _, cols = weights.shape
+    rows = resid.shape[0]
+    groups = n_dp // 2
+    half = groups * rows
+    hidden = gate_w.shape[0]
+    side, group = lax.rem(dp, 2), dp // 2
+    mate = (group * 2 + 1 - side, me)
+
+    def other(j):
+        return lax.rem(group + j, groups)
+
+    def dp_peer(j):
+        return lax.rem(dp + j, n_dp)
+
+    def tensor_peer(j):
+        return lax.rem(me + j, n_tensor)
+
+    def block(g, c):
+        return pl.ds(pl.multiple_of((g * 2 + c) * rows, rows), rows)
+
+    def span(m):
+        return pl.ds(pl.multiple_of(m * cols, cols), cols)
+
+    def w_copies(m):
+        return [
+            pltpu.make_async_copy(w.at[:, span(m)], weights.at[m, i], w_sem.at[m, i])
+            for i, w in enumerate((gate_w, up_w))
+        ]
+
+    for m in range(chunks):
+        for copy in w_copies(m):
+            copy.start()
+
+    barrier = pltpu.get_barrier_semaphore()
+    for j in range(1, n_dp):
+        pl.semaphore_signal(barrier, inc=1, device_id=(dp_peer(j), me), device_id_type=MESH)
+    for j in range(1, n_tensor):
+        pl.semaphore_signal(barrier, inc=1, device_id=(dp, tensor_peer(j)), device_id_type=MESH)
+
+    for i, source in enumerate((gate_all, up_all)):
+        for g in range(groups):
+            paired[i, pl.ds(g * rows, rows)] = source[block(g, 1 - side)]
+            paired[i, pl.ds(half + g * rows, rows)] = source[block(g, side)]
+    pl.semaphore_wait(barrier, n_dp + n_tensor - 2)
+
+    def pair_copy(m):
+        return pltpu.make_async_remote_copy(
+            pair_out.at[m], pair_in.at[m], pair_s.at[m], pair_r.at[m],
+            device_id=mate, device_id_type=MESH,
+        )
+
+    def far_copy(m, j, source):
+        return pltpu.make_async_remote_copy(
+            far_out.at[m, j - 1], far_in.at[m, source], far_s.at[m, j - 1], far_r.at[m, source],
+            device_id=(other(j) * 2 + side, me), device_id_type=MESH,
+        )
+
+    def gain_copy(j, source):
+        return pltpu.make_async_remote_copy(
+            gain_in.at[source], gain_in.at[source], gain_s.at[j - 1], gain_r.at[source],
+            device_id=(dp_peer(j), me), device_id_type=MESH,
+        )
+
+    def coeff_copy(j, source):
+        return pltpu.make_async_remote_copy(
+            coeff_in.at[source], coeff_in.at[source], coeff_s.at[j - 1], coeff_r.at[source],
+            device_id=(dp, tensor_peer(j)), device_id_type=MESH,
+        )
+
+    def product(m):
+        for copy in w_copies(m):
+            copy.wait()
+        part = jnp.dot(paired[0], weights[m, 0], preferred_element_type=jnp.float32)
+        part += jnp.dot(paired[1], weights[m, 1], preferred_element_type=jnp.float32)
+        pair_out[m] = part[:half].astype(jnp.bfloat16)
+        own[m] = part[half:]
+        pair_copy(m).start()
+
+    def pair_sum(m):
+        pair_copy(m).wait_recv()
+        for j in range(1, groups):
+            at = pl.ds(pl.multiple_of(other(j) * rows, rows), rows)
+            total = own[m, at] + pair_in[m, at].astype(jnp.float32)
+            far_out[m, j - 1] = total.astype(jnp.bfloat16)
+            far_copy(m, j, group).start()
+
+    def far_sum(m):
+        at = pl.ds(pl.multiple_of(group * rows, rows), rows)
+        total = own[m, at] + pair_in[m, at].astype(jnp.float32)
+        for j in range(1, groups):
+            far_copy(m, j, other(j)).wait_recv()
+            total += far_in[m, other(j)].astype(jnp.float32)
+        total = total.astype(jnp.bfloat16).astype(jnp.float32)
+        delta[m] = total
+        moved = total * resid[:, span(m)].astype(jnp.float32)
+        gain_in[dp, :, span(m)] = jnp.sum(moved * inv[...], axis=0, keepdims=True)
+        terms = moved * gain[:, span(m)]
+        coeff_in[me] += sum(terms[:, c : c + 128] for c in range(0, cols, 128))
+
+    coeff_in[me] = jnp.zeros(coeff_in.shape[1:], jnp.float32)
+    stages = ((product, 0), (pair_sum, 1), (far_sum, 3))
+
+    def step(s, carry):
+        for stage, lag in stages:
+            @pl.when((s >= lag) & (s < chunks + lag))
+            def _():
+                stage(s - lag)
+        return carry
+
+    lax.fori_loop(0, chunks + stages[-1][1], step, 0)
+
+    for j in range(1, n_tensor):
+        coeff_copy(j, me).start()
+    for j in range(1, n_dp):
+        gain_copy(j, dp).start()
+    for j in range(1, n_tensor):
+        coeff_copy(j, tensor_peer(j)).wait_recv()
+    lanes = coeff_in[0]
+    for t in range(1, n_tensor):
+        lanes += coeff_in[t]
+    coeff = jnp.sum(lanes, axis=1, keepdims=True) / (n_tensor * chunks * cols)
+    inv_v = inv[...]
+    cubed = inv_v * inv_v * inv_v
+
+    for m in range(chunks):
+        at = pl.ds(m * cols, cols)
+        grad[:, at] = (
+            inv_v * gain[:, at] * delta[m] - resid[:, at].astype(jnp.float32) * cubed * coeff
+        ).astype(grad.dtype)
+
+    for j in range(1, n_dp):
+        gain_copy(j, dp_peer(j)).wait_recv()
+    total = gain_in[0]
+    for d in range(1, n_dp):
+        total += gain_in[d]
+    gain_grad[...] = total * scale
+
+    def finish(m, carry):
+        pair_copy(m).wait_send()
+        for j in range(1, groups):
+            far_copy(m, j, group).wait_send()
+        return carry
+
+    lax.fori_loop(0, chunks, finish, 0)
+    for j in range(1, n_tensor):
+        coeff_copy(j, me).wait_send()
+    for j in range(1, n_dp):
+        gain_copy(j, dp).wait_send()
+
+
+def input_gradient(gate_all, up_all, gate_weight, up_weight, resid_rows, inv_rows, gain, scale):
+    total, hidden = gate_all.shape
+    rows, width = resid_rows.shape
+    n_dp, n_tensor = lax.axis_size("dp"), lax.axis_size("tensor")
+    groups = n_dp // 2
+    half = groups * rows
+    cols = 256
+    chunks = width // cols
+    dma = pltpu.SemaphoreType.DMA
+    vmem = pl.BlockSpec(memory_space=pltpu.VMEM)
+    hbm = pl.BlockSpec(memory_space=pl.ANY)
+    return pl.pallas_call(
+        functools.partial(input_kernel, scale),
+        out_shape=[
+            jax.ShapeDtypeStruct((rows, width), jnp.bfloat16),
+            jax.ShapeDtypeStruct((1, width), jnp.float32),
+        ],
+        in_specs=[vmem, vmem, hbm, hbm, vmem, vmem, vmem],
+        out_specs=[vmem, vmem],
+        scratch_shapes=[
+            pltpu.VMEM((2, total, hidden), jnp.bfloat16),
+            pltpu.VMEM((chunks, 2, hidden, cols), jnp.bfloat16),
+            pltpu.VMEM((chunks, half, cols), jnp.bfloat16),
+            pltpu.VMEM((chunks, half, cols), jnp.bfloat16),
+            pltpu.VMEM((chunks, half, cols), jnp.float32),
+            pltpu.VMEM((chunks, max(groups - 1, 1), rows, cols), jnp.bfloat16),
+            pltpu.VMEM((chunks, groups, rows, cols), jnp.bfloat16),
+            pltpu.VMEM((chunks, rows, cols), jnp.float32),
+            pltpu.VMEM((n_dp, 1, width), jnp.float32),
+            pltpu.VMEM((n_tensor, rows, 128), jnp.float32),
+            dma((chunks, 2)),
+            dma((chunks,)),
+            dma((chunks,)),
+            dma((chunks, groups)),
+            dma((chunks, groups)),
+            dma((n_dp,)),
+            dma((n_dp,)),
+            dma((n_tensor,)),
+            dma((n_tensor,)),
+        ],
+        compiler_params=pltpu.CompilerParams(
+            collective_id=1, has_side_effects=True, vmem_limit_bytes=56 * 1024 * 1024
+        ),
+        cost_estimate=pl.CostEstimate(
+            flops=4 * total * width * hidden,
+            bytes_accessed=4 * hidden * width,
+            transcendentals=0,
+        ),
+    )(gate_all, up_all, gate_weight, up_weight, resid_rows, inv_rows, gain)
+
+
 def shards(residual, hidden_cotangent, norm_gain, gate_weight, up_weight):
     width = residual.shape[1]
     slice_width = gate_weight.shape[1]
@@ -231,24 +433,15 @@
     tokens_total = tokens * lax.axis_size("tensor")
     scale = tokens_total ** (-0.5)
     rows_each = tokens_total // lax.axis_size("dp")
-    delta_part = jnp.dot(gate_all, gate_weight, preferred_element_type=jnp.float32) + jnp.dot(
-        up_all, up_weight, preferred_element_type=jnp.float32
-    )
-    delta_rows = scattered_sum(delta_part, "dp")
     gate_grad = (left_product(gate_all, feat_normed) * scale).astype(jnp.bfloat16)
     up_grad = (left_product(up_all, feat_normed) * scale).astype(jnp.bfloat16)
-    delta_f = delta_rows.astype(jnp.bfloat16).astype(jnp.float32)
     row_start = lax.axis_index("dp") * rows_each
-    resid_rows = lax.dynamic_slice_in_dim(feat_resid, row_start, rows_each, 0).astype(jnp.float32)
+    resid_rows = lax.dynamic_slice_in_dim(feat_resid, row_start, rows_each, 0)
     inv_rows = lax.dynamic_slice_in_dim(feat_inv, row_start, rows_each, 0)
-    gain_part = jnp.sum(delta_f * resid_rows * inv_rows, axis=0)
-    coeff_part = jnp.sum(gain_slice * delta_f * resid_rows, axis=1)
-    coeff = lax.psum(coeff_part, "tensor")[:, None] / width
-    gain_total = lax.psum(gain_part, "dp")
-    input_grad = (
-        inv_rows * gain_slice * delta_f - resid_rows * (inv_rows * inv_rows * inv_rows) * coeff
+    input_grad, gain_grad = input_gradient(
+        gate_all, up_all, gate_weight, up_weight, resid_rows, inv_rows, gain_slice[None], scale
     )
-    return (input_grad.astype(jnp.bfloat16), gate_grad, up_grad, gain_total * scale)
+    return (input_grad, gate_grad, up_grad, gain_grad[0])
 
 
 def solution(mesh):

time: 188 us -> 152 us (0.81)
  Pallas kernels: 50.9 us -> 96.1 us
  waiting for transfers between devices: 33.3 us -> 0.01 us
  blocking collectives: 49.2 us -> 24.5 us
  matrix products: 30.8 us -> 13.8 us
  starting transfers between devices: 10.9 us -> 4.21 us
  local copies, waits for them, and re-layouts: 3.87 us -> 8.34 us
  other arithmetic: 7.79 us -> 3.95 us
    pallas_call x0 -> x1, Pallas kernels: none -> 45.1 us  [input_gradient(): pl.pallas_call(functools.partial(input_kernel, scale), out_shape=[jax.Sha...]
    all_to_all x1 -> x0, waiting for transfers between devices: 33.3 us -> none  [scattered_sum(): lax.all_to_all(pieces, axis, split_axis=0, concat_axis=0, tiled=True)]
    psum x2 -> x0, blocking collectives: 25.4 us -> none  [the longest x1 19.7 us: shards(): gain_total = lax.psum(gain_part, 'dp')]
    dot_general x2 -> x0, matrix products: 15.3 us -> none  [the longest x1 8.43 us: shards(): jnp.dot(up_all, up_weight, preferred_element_type=jnp.float32)]
    all_to_all x1 -> x0, starting transfers between devices: 6.65 us -> none  [scattered_sum(): lax.all_to_all(pieces, axis, split_axis=0, concat_axis=0, tiled=True)]
    unnamed x6 -> x8, local copies, waits for them, and re-layouts: 0.01 us -> 2.98 us
    reduce_sum x2 -> x0, other arithmetic: 2.19 us -> none  [the longest x1 1.96 us: scattered_sum(): return jnp.sum(pieces.astype(jnp.float32), axis=0)]
  transfers between devices with their start and end apart: 2 -> 1, of which waited for: 1 -> 0; matrix products, arithmetic and copies ran while one was open for 10% -> 2% of each run, Pallas kernels for 0% -> 0%
where the time goes in v3:
time: 152 us
  Pallas kernels  96.1 us (63%)
  blocking collectives  24.5 us (16%)
  matrix products  13.8 us (9%)
  local copies, waits for them, and re-layouts  8.34 us (5%)
  starting transfers between devices  4.21 us (3%)
  other arithmetic  3.95 us (3%)
    pallas_call x1, Pallas kernels, all_deltas(): pl.pallas_call(functools.partial(delta_kernel, groups, chunks), out_shape...  51 us
    pallas_call x1, Pallas kernels, input_gradient(): pl.pallas_call(functools.partial(input_kernel, scale), out_shape=[jax.Sha...  45.1 us
    all_gather x1, blocking collectives, shards(): feat_inv = lax.all_gather(own_inv, 'tensor', axis=0, tiled=True)[:, None]  24.5 us
    dot_general x2, matrix products, left_product(): lax.dot_general(left, right, (((0,), (0,)), ((), ())), preferred_element_...  13.8 us
    all_to_all x1, starting transfers between devices, shards(): lax.all_to_all(residual, 'tensor', split_axis=1, concat_axis=0, tiled=True)  4.21 us
    all_to_all x1, local copies, waits for them, and re-layouts, shards(): lax.all_to_all(residual, 'tensor', split_axis=1, concat_axis=0, tiled=True)  3.16 us
  transfers between devices with their start and end apart: 1, of which 0 were waited for; matrix products, arithmetic and copies ran while one was open for 2% of the time, Pallas kernels for 0%

profile of v3, /device:TPU:0, one launch (start us, length us, event | category | flops | bytes accessed | tf_op | source)
XLA Modules:
  0.0 151.6 jit_solution(456873190679492707)
XLA Ops:
  0.6 3.2 %copy.15 = bf16[16,4,8,2048]{3,2,0,1:T(8,128)(2,1)} copy(bf16[16,4,8,2048]{3,2,1,0:T(8,128)(2,1)} %bitcast.20) | data formatting | bytes 4194304 | tf_op jit(solution)/shard_map/all_to_all | solution.py:423
  3.8 4.2 %all-to-all-start = ((bf16[128,4,2048]{2,0,1:T(8,128)(2,1)}), bf16[128,4,2048]{2,0,1:T(8,128)(2,1)S(1)}, u32[]{:S(2)}, u32[]{:S(2)}) async-start(bf16[128,4,2048]{2,0,1:T(8,128)(2,1)} %bitcast.21), calls=%async_computation | async-start | bytes 4194304 | tf_op jit(solution)/shard_map/all_to_all | solution.py:423
  8.0 2.1 %multiply_reduce_fusion = f32[128]{0:T(128)S(1)} fusion(bf16[128,8192]{1,0:T(8,128)(2,1)} %param.5), kind=kLoop, calls=%fused_computation.3 | loop fusion | flops 3145600 | bytes 2097664 | tf_op jit(solution)/shard_map/reduce_sum | solution.py:425
  10.1 24.5 %all-gather = f32[4,1,128]{2,1,0:T(1,128)S(1)} all-gather(f32[1,1,128]{2,1,0:T(1,128)S(1)} %rsqrt_bitcast_fusion), channel_id=1, replica_groups=mesh['dp'=8,'tensor'=4] {'tensor'}, dimensions={0}, use_global_device_ids=true | all-gather | bytes 2560 | tf_op jit(solution)/shard_map/all_gather | solution.py:426
  34.6 0.1 dynamic-slice_bitcast_fusion
  34.7 0.7 copy.12.inv
  35.4 0.7 dynamic_slice.9
  36.1 0.0 copy-start.1
  36.1 0.0 all-to-all-done
  36.1 0.7 constant_dynamic-slice_fusion.resid
  36.8 1.9 %multiply_convert_fusion.2.normed = bf16[512,2048]{1,0:T(8,128)(2,1)} fusion(f32[2048]{0:T(1024)S(1)} %dynamic_slice.9, f32[512]{0:T(512)S(1)} %bitcast.24, bf16[128,4,2048]{2,0,1:T(8,128)(2,1)S(1)} %all-to-all-done), kind=kLoop, calls=%fused_computation.2 | loop fusion | flops 4194304 | bytes 4204544 | tf_op jit(solution)/shard_map/convert_element_type | solution.py:431
  38.7 0.0 copy-done.1
  38.7 0.0 copy-start
  38.7 51.0 %shard_map.84 = (bf16[512,1792]{1,0:T(8,128)(2,1)}, bf16[512,1792]{1,0:T(8,128)(2,1)}) custom-call(bf16[512,2048]{1,0:T(8,128)(2,1)} %multiply_convert_fusion.2.normed, bf16[128,1792]{1,0:T(8,128)(2,1)} %cot.1, bf16[1792,2048]{1,0:T(8,128)(2,1)} %gate_w.3, bf16[1792,2048]{1,0:T(8,128)(2,1)} %up_w.3), custom_call_target="tpu_custom_call" | custom-call | flops 7516192768 | bytes 14680064 | tf_op jit(solution)/shard_map/pallas_call | solution.py:178
  89.7 0.0 copy-done
  89.7 0.0 copy-start.2
  89.7 7.7 %multiply_convert_fusion = bf16[1792,2048]{1,0:T(8,128)(2,1)} fusion(bf16[512,1792]{1,0:T(8,128)(2,1)} %get-tuple-element.9.up_all, bf16[512,2048]{1,0:T(8,128)(2,1)S(1)} %copy-done), kind=kOutput, calls=%fused_computation | convolution fusion | flops 3765436416 | bytes 11272192 | tf_op jit(solution)/shard_map/dot_general | solution.py:26
  97.4 0.0 copy-done.2
  97.4 6.1 %multiply_convert_fusion.1 = bf16[1792,2048]{1,0:T(8,128)(2,1)} fusion(bf16[512,1792]{1,0:T(8,128)(2,1)S(1)} %copy-done.2, bf16[512,2048]{1,0:T(8,128)(2,1)S(1)} %copy-done), kind=kOutput, calls=%fused_computation.1 | convolution fusion | flops 3765436416 | bytes 11272192 | tf_op jit(solution)/shard_map/dot_general | solution.py:26
  103.5 45.1 %shard_map.85 = (bf16[64,2048]{1,0:T(8,128)(2,1)}, f32[1,2048]{1,0:T(1,128)}) custom-call(bf16[512,1792]{1,0:T(8,128)(2,1)} %get-tuple-element.8.gate_all, bf16[512,1792]{1,0:T(8,128)(2,1)} %get-tuple-element.9.up_all, bf16[1792,2048]{1,0:T(8,128)(2,1)} %gate_w.3, bf16[1792,2048]{1,0:T(8,128)(2,1)} %up_w.3, ...), custom_call_target="tpu_custom_call" | custom-call | flops 7516192768 | bytes 14680064 | tf_op jit(solution)/shard_map/pallas_call | solution.py:379
  148.6 1.7 %copy.18 = bf16[64,2048]{1,0:T(8,128)(2,1)} copy(bf16[64,2048]{1,0:T(8,128)(2,1)} %get-tuple-element.16) | data formatting | bytes 524288
  150.3 1.3 copy.19
  (1 shorter events, 0.0 us)
Async XLA Ops:
  3.8 32.3 %all-to-all-start = ((bf16[128,4,2048]{2,0,1:T(8,128)(2,1)}), bf16[128,4,2048]{2,0,1:T(8,128)(2,1)S(1)}, u32[]{:S(2)}, u32[]{:S(2)}) async-start(bf16[128,4,2048]{2,0,1:T(8,128)(2,1)} %bitcast.21), calls=%async_computation | async-start | bytes 4194304 | tf_op jit(solution)/shard_map/all_to_all | solution.py:423
  36.1 2.6 %copy-start.1 = (f32[2048]{0:T(1024)}, f32[2048]{0:T(1024)S(1)}, u32[]{:S(2)}) copy-start(f32[2048]{0:T(1024)S(1)} %dynamic_slice.9) | copy-start | bytes 24580
  38.7 51.1 %copy-start = (bf16[512,2048]{1,0:T(8,128)(2,1)S(1)}, bf16[512,2048]{1,0:T(8,128)(2,1)}, u32[]{:S(2)}) copy-start(bf16[512,2048]{1,0:T(8,128)(2,1)} %multiply_convert_fusion.2.normed) | copy-start | bytes 6291460
  89.7 7.7 %copy-start.2 = (bf16[512,1792]{1,0:T(8,128)(2,1)S(1)}, bf16[512,1792]{1,0:T(8,128)(2,1)}, u32[]{:S(2)}) copy-start(bf16[512,1792]{1,0:T(8,128)(2,1)} %get-tuple-element.8.gate_all) | copy-start | bytes 5505028

commit v4 on v3

--- a/solution.py
+++ b/solution.py
@@ -32,8 +32,8 @@
 
 
 def delta_kernel(
-    groups, chunks, normed, cot, gate_w, up_w, gate_all, up_all,
-    paired, weights, pair_out, pair_in, own, far_out, far_in,
+    groups, chunks, residual, all_gain, cot, gate_w, up_w, gate_all, up_all, normed, inv_all,
+    norm_out, norm_s, norm_r, paired, weights, pair_out, pair_in, own, far_out, far_in,
     w_sem, pair_s, pair_r, far_s, far_r, peer_s, peer_r, sib_s, sib_r,
 ):
     me = lax.axis_index("tensor")
@@ -71,11 +71,47 @@
         pl.semaphore_signal(
             barrier, inc=1, device_id=(dp, other(j) * 2 + core), device_id_type=MESH
         )
+        pl.semaphore_signal(
+            barrier, inc=1, device_id=(dp, other(j) * 2 + sib_core), device_id_type=MESH
+        )
+
+    n_tensor, _, width = norm_out.shape
+    squares = jnp.zeros((rows, 1), jnp.float32)
+    for p in range(n_tensor):
+        part = residual[:, pl.ds(p * width, width)].astype(jnp.float32)
+        squares += jnp.sum(part * part, axis=1, keepdims=True)
+    inv = lax.rsqrt(squares / (n_tensor * width) + 1e-05)
+    for p in range(n_tensor):
+        at = pl.ds(p * width, width)
+        norm_out[p] = (residual[:, at].astype(jnp.float32) * inv * all_gain[:, at]).astype(
+            jnp.bfloat16
+        )
+    normed[block(group, core)] = norm_out[me]
+    inv_all[block(group, core)] = jnp.broadcast_to(inv, (rows, 128))
+    pl.semaphore_wait(barrier, n_tensor - 1)
+
+    def norm_copies(j, source):
+        peer = lax.rem(me + j, n_tensor)
+        at = pl.ds(pl.multiple_of(source * rows, rows), rows)
+        return [
+            pltpu.make_async_remote_copy(
+                part, whole.at[at], norm_s.at[j - 1, i], norm_r.at[source, i],
+                device_id=(dp, peer), device_id_type=MESH,
+            )
+            for i, (part, whole) in enumerate(
+                ((norm_out.at[peer], normed), (inv_all.at[at], inv_all))
+            )
+        ]
+
+    for i in range(2):
+        for j in range(1, n_tensor):
+            norm_copies(j, me)[i].start()
+    for j in range(1, n_tensor):
+        norm_copies(j, lax.rem(me + j, n_tensor))[0].wait_recv()
 
     for g in range(groups):
         paired[pl.ds(g * rows, rows)] = normed[block(g, sib_core)]
         paired[pl.ds(half + g * rows, rows)] = normed[block(g, core)]
-    pl.semaphore_wait(barrier, groups)
 
     def pair_copy(k):
         return pltpu.make_async_remote_copy(
@@ -163,11 +199,17 @@
         return carry
 
     lax.fori_loop(0, chunks, finish, 0)
-
-
-def all_deltas(normed, cot, gate_weight, up_weight):
+    for j in range(1, n_tensor):
+        norm_copies(j, lax.rem(me + j, n_tensor))[1].wait_recv()
+        for copy in norm_copies(j, me):
+            copy.wait_send()
+
+
+def all_deltas(residual, gain, cot, gate_weight, up_weight):
     rows, hidden = cot.shape
-    total, width = normed.shape
+    width = gate_weight.shape[1]
+    n_tensor = lax.axis_size("tensor")
+    total = rows * n_tensor
     groups = total // rows // 2
     chunks = hidden // 256 if hidden % 256 == 0 else 1
     cols = hidden // chunks
@@ -177,10 +219,17 @@
     flops = 4 * total * width * hidden
     return pl.pallas_call(
         functools.partial(delta_kernel, groups, chunks),
-        out_shape=[jax.ShapeDtypeStruct((total, hidden), jnp.bfloat16)] * 2,
-        in_specs=[vmem, vmem, pl.BlockSpec(memory_space=pl.ANY), pl.BlockSpec(memory_space=pl.ANY)],
-        out_specs=[vmem, vmem],
+        out_shape=[jax.ShapeDtypeStruct((total, hidden), jnp.bfloat16)] * 2
+        + [
+            jax.ShapeDtypeStruct((total, width), jnp.bfloat16),
+            jax.ShapeDtypeStruct((total, 128), jnp.float32),
+        ],
+        in_specs=[vmem, vmem, vmem, pl.BlockSpec(memory_space=pl.ANY), pl.BlockSpec(memory_space=pl.ANY)],
+        out_specs=[vmem] * 4,
         scratch_shapes=[
+            pltpu.VMEM((n_tensor, rows, width), jnp.bfloat16),
+            dma((n_tensor, 2)),
+            dma((n_tensor, 2)),
             pltpu.VMEM((total, width), jnp.bfloat16),
             pltpu.VMEM((chunks, 2 * cols, width), jnp.bfloat16),
             pltpu.VMEM((chunks, half, 2 * cols), jnp.bfloat16),
@@ -204,11 +253,11 @@
         cost_estimate=pl.CostEstimate(
             flops=flops, bytes_accessed=4 * hidden * width, transcendentals=0
         ),
-    )(normed, cot, gate_weight, up_weight)
+    )(residual, gain, cot, gate_weight, up_weight)
 
 
 def input_kernel(
-    scale, gate_all, up_all, gate_w, up_w, resid, inv, gain, grad, gain_grad,
+    scale, gate_all, up_all, gate_w, up_w, normed, inv, gain, grad, gain_grad,
     paired, weights, pair_out, pair_in, own, far_out, far_in, delta, gain_in, coeff_in,
     w_sem, pair_s, pair_r, far_s, far_r, gain_s, gain_r, coeff_s, coeff_r,
 ):
@@ -216,7 +265,7 @@
     dp = lax.axis_index("dp")
     n_tensor, n_dp = coeff_in.shape[0], gain_in.shape[0]
     chunks, _, _, cols = weights.shape
-    rows = resid.shape[0]
+    rows = normed.shape[0]
     groups = n_dp // 2
     half = groups * rows
     hidden = gate_w.shape[0]
@@ -309,9 +358,8 @@
             total += far_in[m, other(j)].astype(jnp.float32)
         total = total.astype(jnp.bfloat16).astype(jnp.float32)
         delta[m] = total
-        moved = total * resid[:, span(m)].astype(jnp.float32)
-        gain_in[dp, :, span(m)] = jnp.sum(moved * inv[...], axis=0, keepdims=True)
-        terms = moved * gain[:, span(m)]
+        terms = total * normed[:, span(m)].astype(jnp.float32)
+        gain_in[dp, :, span(m)] = jnp.sum(terms, axis=0, keepdims=True) / gain[:, span(m)]
         coeff_in[me] += sum(terms[:, c : c + 128] for c in range(0, cols, 128))
 
     coeff_in[me] = jnp.zeros(coeff_in.shape[1:], jnp.float32)
@@ -336,13 +384,12 @@
     for t in range(1, n_tensor):
         lanes += coeff_in[t]
     coeff = jnp.sum(lanes, axis=1, keepdims=True) / (n_tensor * chunks * cols)
-    inv_v = inv[...]
-    cubed = inv_v * inv_v * inv_v
+    inv_v = inv[:, :1]
 
     for m in range(chunks):
         at = pl.ds(m * cols, cols)
         grad[:, at] = (
-            inv_v * gain[:, at] * delta[m] - resid[:, at].astype(jnp.float32) * cubed * coeff
+            inv_v * (gain[:, at] * delta[m] - normed[:, at].astype(jnp.float32) / gain[:, at] * coeff)
         ).astype(grad.dtype)
 
     for j in range(1, n_dp):
@@ -365,9 +412,9 @@
         gain_copy(j, dp).wait_send()
 
 
-def input_gradient(gate_all, up_all, gate_weight, up_weight, resid_rows, inv_rows, gain, scale):
+def input_gradient(gate_all, up_all, gate_weight, up_weight, normed_rows, inv_rows, gain, scale):
     total, hidden = gate_all.shape
-    rows, width = resid_rows.shape
+    rows, width = normed_rows.shape
     n_dp, n_tensor = lax.axis_size("dp"), lax.axis_size("tensor")
     groups = n_dp // 2
     half = groups * rows
@@ -413,33 +460,28 @@
             bytes_accessed=4 * hidden * width,
             transcendentals=0,
         ),
-    )(gate_all, up_all, gate_weight, up_weight, resid_rows, inv_rows, gain)
+    )(gate_all, up_all, gate_weight, up_weight, normed_rows, inv_rows, gain)
 
 
 def shards(residual, hidden_cotangent, norm_gain, gate_weight, up_weight):
-    width = residual.shape[1]
     slice_width = gate_weight.shape[1]
     tokens = residual.shape[0]
-    feat_resid = lax.all_to_all(residual, "tensor", split_axis=1, concat_axis=0, tiled=True)
-    resid_f = residual.astype(jnp.float32)
-    own_inv = lax.rsqrt(jnp.mean(resid_f * resid_f, axis=-1) + 1e-05)
-    feat_inv = lax.all_gather(own_inv, "tensor", axis=0, tiled=True)[:, None]
-    feat_f = feat_resid.astype(jnp.float32)
     gain_slice = lax.dynamic_slice_in_dim(
         norm_gain, lax.axis_index("tensor") * slice_width, slice_width
     )
-    feat_normed = (feat_f * feat_inv * gain_slice).astype(jnp.bfloat16)
-    gate_all, up_all = all_deltas(feat_normed, hidden_cotangent, gate_weight, up_weight)
+    gate_all, up_all, feat_normed, feat_inv = all_deltas(
+        residual, norm_gain[None], hidden_cotangent, gate_weight, up_weight
+    )
     tokens_total = tokens * lax.axis_size("tensor")
     scale = tokens_total ** (-0.5)
     rows_each = tokens_total // lax.axis_size("dp")
     gate_grad = (left_product(gate_all, feat_normed) * scale).astype(jnp.bfloat16)
     up_grad = (left_product(up_all, feat_normed) * scale).astype(jnp.bfloat16)
     row_start = lax.axis_index("dp") * rows_each
-    resid_rows = lax.dynamic_slice_in_dim(feat_resid, row_start, rows_each, 0)
+    normed_rows = lax.dynamic_slice_in_dim(feat_normed, row_start, rows_each, 0)
     inv_rows = lax.dynamic_slice_in_dim(feat_inv, row_start, rows_each, 0)
     input_grad, gain_grad = input_gradient(
-        gate_all, up_all, gate_weight, up_weight, resid_rows, inv_rows, gain_slice[None], scale
+        gate_all, up_all, gate_weight, up_weight, normed_rows, inv_rows, gain_slice[None], scale
     )
     return (input_grad, gate_grad, up_grad, gain_grad[0])
 

time: 152 us -> 142 us (0.934)
  Pallas kernels: 96.1 us -> 123 us
  blocking collectives: 24.5 us -> 0 us
  starting transfers between devices: 4.21 us -> 0 us
  other arithmetic: 3.95 us -> 0 us
  local copies, waits for them, and re-layouts: 8.34 us -> 5.67 us
  matrix products: 13.8 us -> 12.2 us
    pallas_call x1, Pallas kernels: 51 us -> 78.7 us  [all_deltas(): pl.pallas_call(functools.partial(delta_kernel, groups, chunks), out_shape...]
    all_gather x1 -> x0, blocking collectives: 24.5 us -> none  [shards(): feat_inv = lax.all_gather(own_inv, 'tensor', axis=0, tiled=True)[:, None]]
    all_to_all x1 -> x0, starting transfers between devices: 4.21 us -> none  [shards(): lax.all_to_all(residual, 'tensor', split_axis=1, concat_axis=0, tiled=True)]
    all_to_all x1 -> x0, local copies, waits for them, and re-layouts: 3.16 us -> none  [shards(): lax.all_to_all(residual, 'tensor', split_axis=1, concat_axis=0, tiled=True)]
    reduce_sum x1 -> x0, other arithmetic: 2.08 us -> none  [shards(): own_inv = lax.rsqrt(jnp.mean(resid_f * resid_f, axis=-1) + 1e-05)]
    convert_element_type x1 -> x0, other arithmetic: 1.86 us -> none  [shards(): feat_normed = (feat_f * feat_inv * gain_slice).astype(jnp.bfloat16)]
    unnamed x8 -> x12, local copies, waits for them, and re-layouts: 2.98 us -> 1.32 us
    dot_general x2, matrix products: 13.8 us -> 12.2 us  [left_product(): lax.dot_general(left, right, (((0,), (0,)), ((), ())), preferred_element_...]
  transfers between devices with their start and end apart: 1 -> 0, of which waited for: 0 -> 0; matrix products, arithmetic and copies ran while one was open for 2% -> 0% of each run, Pallas kernels for 0% -> 0%
where the time goes in v4:
time: 142 us; the launch traced here: 141 us
  Pallas kernels  123 us (87%)
  matrix products  12.2 us (9%)
  local copies, waits for them, and re-layouts  5.67 us (4%)
    pallas_call x1, Pallas kernels, all_deltas(): pl.pallas_call(functools.partial(delta_kernel, groups, chunks), out_shape...  78.7 us
    pallas_call x1, Pallas kernels, input_gradient(): pl.pallas_call(functools.partial(input_kernel, scale), out_shape=[jax.Sha...  44.3 us
    dot_general x2, matrix products, left_product(): lax.dot_general(left, right, (((0,), (0,)), ((), ())), preferred_element_...  12.2 us

profile of v4, /device:TPU:0, one launch (start us, length us, event | category | flops | bytes accessed | tf_op | source)
XLA Modules:
  0.0 141.5 jit_solution(4444444290255503416)
XLA Ops:
  0.6 1.3 dynamic_slice.11
  1.9 78.7 %shard_map.84 = (bf16[512,1792]{1,0:T(8,128)(2,1)}, bf16[512,1792]{1,0:T(8,128)(2,1)}, bf16[512,2048]{1,0:T(8,128)(2,1)}, f32[512,128]{1,0:T(8,128)}) custom-call(bf16[128,8192]{1,0:T(8,128)(2,1)} %residual.1, f32[1,8192]{1,0:T(1,128)} %bitcast.9, bf16[128,1792]{1,0:T(8,128)(2,1)} %cot.1, bf16[1792,2048]{1,0:T(8,128)(2,1)} %gate_w.3, bf16[1792,2048]{1,0:T(8,128)(2,1)} %up_w.3), custom_call_target="tpu_custom_call" | custom-call | flops 7516192768 | bytes 14680064 | tf_op jit(solution)/shard_map/pallas_call | solution.py:220
  80.6 1.4 constant_dynamic-slice_fusion.inv
  82.0 1.7 %constant_dynamic-slice_fusion.1.normed = bf16[64,2048]{1,0:T(8,128)(2,1)} fusion(bf16[512,2048]{1,0:T(8,128)(2,1)} %get-tuple-element.12, s32[]{:T(128)S(6)} %select_n.7), kind=kLoop, calls=%fused_computation.3 | loop fusion | bytes 524292 | tf_op jit(solution)/shard_map/dynamic_slice | solution.py:481
  83.7 0.0 copy-start.1
  83.7 0.0 copy-start.4
  83.7 44.3 %shard_map.85 = (bf16[64,2048]{1,0:T(8,128)(2,1)}, f32[1,2048]{1,0:T(1,128)}) custom-call(bf16[512,1792]{1,0:T(8,128)(2,1)} %get-tuple-element.10.gate_all, bf16[512,1792]{1,0:T(8,128)(2,1)} %get-tuple-element.11.up_all, bf16[1792,2048]{1,0:T(8,128)(2,1)} %gate_w.3, bf16[1792,2048]{1,0:T(8,128)(2,1)} %up_w.3, ...), custom_call_target="tpu_custom_call" | custom-call | flops 7516192768 | bytes 14680064 | tf_op jit(solution)/shard_map/pallas_call | solution.py:426
  128.0 0.0 copy-done.1
  128.0 0.0 copy-done.4
  128.0 0.0 copy-start.3
  128.0 6.1 %multiply_convert_fusion = bf16[1792,2048]{1,0:T(8,128)(2,1)} fusion(bf16[512,1792]{1,0:T(8,128)(2,1)S(1)} %copy-done.4, bf16[512,2048]{1,0:T(8,128)(2,1)S(1)} %copy-done.1), kind=kOutput, calls=%fused_computation | convolution fusion | flops 3765436416 | bytes 11272192 | tf_op jit(solution)/shard_map/dot_general | solution.py:26
  134.1 0.0 copy-done.3
  134.1 0.0 copy-start
  134.1 0.0 copy-start.2
  134.1 6.1 %multiply_convert_fusion.1 = bf16[1792,2048]{1,0:T(8,128)(2,1)} fusion(bf16[512,1792]{1,0:T(8,128)(2,1)S(1)} %copy-done.3, bf16[512,2048]{1,0:T(8,128)(2,1)S(1)} %copy-done.1), kind=kOutput, calls=%fused_computation.1 | convolution fusion | flops 3765436416 | bytes 11272192 | tf_op jit(solution)/shard_map/dot_general | solution.py:26
  140.2 0.0 copy-done
  140.2 0.7 copy.11
  140.9 0.0 copy-done.2
  140.9 0.6 copy.12
Async XLA Ops:
  83.7 44.3 %copy-start.1 = (bf16[512,2048]{1,0:T(8,128)(2,1)S(1)}, bf16[512,2048]{1,0:T(8,128)(2,1)}, u32[]{:S(2)}) copy-start(bf16[512,2048]{1,0:T(8,128)(2,1)} %get-tuple-element.12) | copy-start | bytes 6291460
  83.7 44.3 %copy-start.4 = (bf16[512,1792]{1,0:T(8,128)(2,1)S(1)}, bf16[512,1792]{1,0:T(8,128)(2,1)}, u32[]{:S(2)}) copy-start(bf16[512,1792]{1,0:T(8,128)(2,1)} %get-tuple-element.11.up_all) | copy-start | bytes 5505028
  128.0 6.1 %copy-start.3 = (bf16[512,1792]{1,0:T(8,128)(2,1)S(1)}, bf16[512,1792]{1,0:T(8,128)(2,1)}, u32[]{:S(2)}) copy-start(bf16[512,1792]{1,0:T(8,128)(2,1)} %get-tuple-element.10.gate_all) | copy-start | bytes 5505028
  134.1 6.1 %copy-start = (bf16[64,2048]{1,0:T(8,128)(2,1)S(1)}, bf16[64,2048]{1,0:T(8,128)(2,1)}, u32[]{:S(2)}) copy-start(bf16[64,2048]{1,0:T(8,128)(2,1)} %get-tuple-element.20) | copy-start | bytes 786436
  134.1 6.8 %copy-start.2 = (f32[1,2048]{1,0:T(1,128)S(1)}, f32[1,2048]{1,0:T(1,128)}, u32[]{:S(2)}) copy-start(f32[1,2048]{1,0:T(1,128)} %get-tuple-element.15) | copy-start | bytes 24580

commit v5 on v4

--- a/solution.py
+++ b/solution.py
@@ -81,13 +81,12 @@
         part = residual[:, pl.ds(p * width, width)].astype(jnp.float32)
         squares += jnp.sum(part * part, axis=1, keepdims=True)
     inv = lax.rsqrt(squares / (n_tensor * width) + 1e-05)
-    for p in range(n_tensor):
-        at = pl.ds(p * width, width)
-        norm_out[p] = (residual[:, at].astype(jnp.float32) * inv * all_gain[:, at]).astype(
-            jnp.bfloat16
-        )
-    normed[block(group, core)] = norm_out[me]
-    inv_all[block(group, core)] = jnp.broadcast_to(inv, (rows, 128))
+
+    def normalize(p):
+        at = pl.ds(pl.multiple_of(p * width, width), width)
+        return (residual[:, at].astype(jnp.float32) * inv * all_gain[:, at]).astype(jnp.bfloat16)
+
+    inv_all[me] = jnp.transpose(jnp.broadcast_to(inv, (rows, 128)))[:8]
     pl.semaphore_wait(barrier, n_tensor - 1)
 
     def norm_copies(j, source):
@@ -95,17 +94,21 @@
         at = pl.ds(pl.multiple_of(source * rows, rows), rows)
         return [
             pltpu.make_async_remote_copy(
-                part, whole.at[at], norm_s.at[j - 1, i], norm_r.at[source, i],
+                part, whole, norm_s.at[j - 1, i], norm_r.at[source, i],
                 device_id=(dp, peer), device_id_type=MESH,
             )
             for i, (part, whole) in enumerate(
-                ((norm_out.at[peer], normed), (inv_all.at[at], inv_all))
+                ((norm_out.at[peer], normed.at[at]), (inv_all.at[source], inv_all.at[source]))
             )
         ]
 
-    for i in range(2):
-        for j in range(1, n_tensor):
-            norm_copies(j, me)[i].start()
+    for j in sorted(range(1, n_tensor), key=lambda j: abs(2 * j - n_tensor)):
+        peer = lax.rem(me + j, n_tensor)
+        norm_out[peer] = normalize(peer)
+        norm_copies(j, me)[0].start()
+    normed[block(group, core)] = normalize(me)
+    for j in range(1, n_tensor):
+        norm_copies(j, me)[1].start()
     for j in range(1, n_tensor):
         norm_copies(j, lax.rem(me + j, n_tensor))[0].wait_recv()
 
@@ -222,7 +225,7 @@
         out_shape=[jax.ShapeDtypeStruct((total, hidden), jnp.bfloat16)] * 2
         + [
             jax.ShapeDtypeStruct((total, width), jnp.bfloat16),
-            jax.ShapeDtypeStruct((total, 128), jnp.float32),
+            jax.ShapeDtypeStruct((n_tensor, 8, rows), jnp.float32),
         ],
         in_specs=[vmem, vmem, vmem, pl.BlockSpec(memory_space=pl.ANY), pl.BlockSpec(memory_space=pl.ANY)],
         out_specs=[vmem] * 4,
@@ -472,6 +475,7 @@
     gate_all, up_all, feat_normed, feat_inv = all_deltas(
         residual, norm_gain[None], hidden_cotangent, gate_weight, up_weight
     )
+    feat_inv = feat_inv[:, 0].reshape(-1, 1)
     tokens_total = tokens * lax.axis_size("tensor")
     scale = tokens_total ** (-0.5)
     rows_each = tokens_total // lax.axis_size("dp")

time: 142 us -> 141 us (level)
  no operation moved by 1% of the time
where the time goes in v5:
time: 141 us
  Pallas kernels  122 us (87%)
  matrix products  12.2 us (9%)
  local copies, waits for them, and re-layouts  5.79 us (4%)
    pallas_call x1, Pallas kernels, all_deltas(): pl.pallas_call(functools.partial(delta_kernel, groups, chunks), out_shape...  78.1 us
    pallas_call x1, Pallas kernels, input_gradient(): pl.pallas_call(functools.partial(input_kernel, scale), out_shape=[jax.Sha...  44.3 us
    dot_general x2, matrix products, left_product(): lax.dot_general(left, right, (((0,), (0,)), ((), ())), preferred_element_...  12.2 us

profile of v5, /device:TPU:0, one launch (start us, length us, event | category | flops | bytes accessed | tf_op | source)
XLA Modules:
  0.0 141.0 jit_solution(4840222096838011559)
XLA Ops:
  0.6 1.3 dynamic_slice.11
  1.9 78.1 %shard_map.84 = (bf16[512,1792]{1,0:T(8,128)(2,1)}, bf16[512,1792]{1,0:T(8,128)(2,1)}, bf16[512,2048]{1,0:T(8,128)(2,1)}, f32[4,8,128]{2,1,0:T(8,128)}) custom-call(bf16[128,8192]{1,0:T(8,128)(2,1)} %residual.1, f32[1,8192]{1,0:T(1,128)} %bitcast.11, bf16[128,1792]{1,0:T(8,128)(2,1)} %cot.1, bf16[1792,2048]{1,0:T(8,128)(2,1)} %gate_w.3, bf16[1792,2048]{1,0:T(8,128)(2,1)} %up_w.3), custom_call_target="tpu_custom_call" | custom-call | flops 7516192768 | bytes 14680064 | tf_op jit(solution)/shard_map/pallas_call | solution.py:223
  80.0 0.7 slice_bitcast_fusion
  80.8 0.1 constant_dynamic-slice_fusion
  80.8 0.7 copy.10.inv
  81.5 1.7 %constant_dynamic-slice_fusion.1.normed = bf16[64,2048]{1,0:T(8,128)(2,1)} fusion(bf16[512,2048]{1,0:T(8,128)(2,1)} %get-tuple-element.12, s32[]{:T(128)S(6)} %select_n.7), kind=kLoop, calls=%fused_computation.4 | loop fusion | bytes 524292 | tf_op jit(solution)/shard_map/dynamic_slice | solution.py:485
  83.2 0.0 copy-start.1
  83.2 0.0 copy-start.4
  83.2 44.3 %shard_map.85 = (bf16[64,2048]{1,0:T(8,128)(2,1)}, f32[1,2048]{1,0:T(1,128)}) custom-call(bf16[512,1792]{1,0:T(8,128)(2,1)} %get-tuple-element.10.gate_all, bf16[512,1792]{1,0:T(8,128)(2,1)} %get-tuple-element.11.up_all, bf16[1792,2048]{1,0:T(8,128)(2,1)} %gate_w.3, bf16[1792,2048]{1,0:T(8,128)(2,1)} %up_w.3, ...), custom_call_target="tpu_custom_call" | custom-call | flops 7516192768 | bytes 14680064 | tf_op jit(solution)/shard_map/pallas_call | solution.py:429
  127.5 0.0 copy-done.1
  127.5 0.0 copy-done.4
  127.5 0.0 copy-start.3
  127.5 6.1 %multiply_convert_fusion = bf16[1792,2048]{1,0:T(8,128)(2,1)} fusion(bf16[512,1792]{1,0:T(8,128)(2,1)S(1)} %copy-done.4, bf16[512,2048]{1,0:T(8,128)(2,1)S(1)} %copy-done.1), kind=kOutput, calls=%fused_computation | convolution fusion | flops 3765436416 | bytes 11272192 | tf_op jit(solution)/shard_map/dot_general | solution.py:26
  133.6 0.0 copy-done.3
  133.6 0.0 copy-start
  133.6 0.0 copy-start.2
  133.6 6.1 %multiply_convert_fusion.1 = bf16[1792,2048]{1,0:T(8,128)(2,1)} fusion(bf16[512,1792]{1,0:T(8,128)(2,1)S(1)} %copy-done.3, bf16[512,2048]{1,0:T(8,128)(2,1)S(1)} %copy-done.1), kind=kOutput, calls=%fused_computation.1 | convolution fusion | flops 3765436416 | bytes 11272192 | tf_op jit(solution)/shard_map/dot_general | solution.py:26
  139.7 0.0 copy-done
  139.7 0.7 copy.13
  140.4 0.0 copy-done.2
  140.4 0.6 copy.14
Async XLA Ops:
  83.2 44.3 %copy-start.1 = (bf16[512,2048]{1,0:T(8,128)(2,1)S(1)}, bf16[512,2048]{1,0:T(8,128)(2,1)}, u32[]{:S(2)}) copy-start(bf16[512,2048]{1,0:T(8,128)(2,1)} %get-tuple-element.12) | copy-start | bytes 6291460
  83.2 44.3 %copy-start.4 = (bf16[512,1792]{1,0:T(8,128)(2,1)S(1)}, bf16[512,1792]{1,0:T(8,128)(2,1)}, u32[]{:S(2)}) copy-start(bf16[512,1792]{1,0:T(8,128)(2,1)} %get-tuple-element.11.up_all) | copy-start | bytes 5505028
  127.5 6.1 %copy-start.3 = (bf16[512,1792]{1,0:T(8,128)(2,1)S(1)}, bf16[512,1792]{1,0:T(8,128)(2,1)}, u32[]{:S(2)}) copy-start(bf16[512,1792]{1,0:T(8,128)(2,1)} %get-tuple-element.10.gate_all) | copy-start | bytes 5505028
  133.6 6.1 %copy-start = (bf16[64,2048]{1,0:T(8,128)(2,1)S(1)}, bf16[64,2048]{1,0:T(8,128)(2,1)}, u32[]{:S(2)}) copy-start(bf16[64,2048]{1,0:T(8,128)(2,1)} %get-tuple-element.20) | copy-start | bytes 786436
  133.6 6.8 %copy-start.2 = (f32[1,2048]{1,0:T(1,128)S(1)}, f32[1,2048]{1,0:T(1,128)}, u32[]{:S(2)}) copy-start(f32[1,2048]{1,0:T(1,128)} %get-tuple-element.15) | copy-start | bytes 24580
